TPU v7x, 256 devices: a whole 4x4x8 slice. The times are simulated.
256 devices in a mesh: row: 16 (over x, y), col: 16 (over z, core).
Axes of the slice: x: 4, y: 4, z: 8, core: 2. Of those that a mesh axis runs over, the one named last changes fastest.
Arguments:
- patches: bfloat16 [4096, 3072], P('row', 'col'), may hold values from -47 to 47
- norm_gain: float32 [3072], P('col'), may hold values from 0.1 to 1.9
- up_weight: bfloat16 [3072, 12288], P('row', 'col'), may hold values from -0.109375 to 0.109375
- up_bias: float32 [12288], P('col'), may hold values from -3 to 3
- down_weight: bfloat16 [12288, 3072], P('col', 'row'), may hold values from -0.0546875 to 0.0546875
- down_bias: float32 [3072], P('col'), may hold values from -3 to 3
- cotangent: bfloat16 [4096, 3072], P('row', 'col'), may hold values from -6 to 6
Outputs:
- mixed: bfloat16 [4096, 3072], P('row', 'col')
- patch_grad: bfloat16 [4096, 3072], P('row', 'col')
- gain_grad: float32 [3072], P('col')
- up_weight_grad: bfloat16 [3072, 12288], P('row', 'col')
- up_bias_grad: float32 [12288], P('col')
- down_weight_grad: bfloat16 [12288, 3072], P('col', 'row')
- down_bias_grad: float32 [3072], P('row')
All inputs are finite; a program needn't handle non-finite values.
Results may differ from a plain program's by a relative error of at most 0.023.
Values may be sent and summed in bfloat16 or wider, within the bound.
A program may use at most 64 MiB of HBM per device.

v0:
```python
import math

import jax
import jax.numpy as jnp
from jax import lax
from jax.sharding import PartitionSpec as P

D = 3072


def gelu_slope(pre_act):
    cdf_part = 0.5 * (1.0 + lax.erf(pre_act * 0.7071067811865476))
    return cdf_part + pre_act * jnp.exp(-0.5 * pre_act * pre_act) * 0.3989422804014327


def contract_last(left, right):
    return lax.dot_general(
        left, right, (((1,), (1,)), ((), ())), preferred_element_type=jnp.float32
    )


def contract_first(left, right):
    return lax.dot_general(
        left, right, (((0,), (0,)), ((), ())), preferred_element_type=jnp.float32
    )


def on_device(patches, norm_gain, up_weight, up_bias, down_weight, down_bias, cotangent):
    rows_here = patches.shape[0]
    grad_scale = 1.0 / math.sqrt(rows_here * lax.axis_size("row"))
    inputs = patches.astype(jnp.float32)
    row_sum = lax.psum(jnp.sum(inputs, axis=1), "col")
    row_mean = row_sum / D
    centred = inputs - row_mean[:, None]
    row_var = lax.psum(jnp.sum(centred * centred, axis=1), "col") / D
    inv_std = lax.rsqrt(row_var + 1e-06)[:, None]
    normed = centred * inv_std
    normed_bf = (normed * norm_gain[None, :]).astype(jnp.bfloat16)
    normed_rows = lax.all_gather(normed_bf, "col", axis=1, tiled=True)
    up_panel = lax.all_gather(up_weight, "row", axis=0, tiled=True)
    down_panel = lax.all_gather(down_weight, "row", axis=1, tiled=True)
    pre_act = jnp.dot(normed_rows, up_panel, preferred_element_type=jnp.float32) + up_bias[None, :]
    hidden = jax.nn.gelu(pre_act, approximate=False).astype(jnp.bfloat16)
    out_terms = jnp.dot(hidden, down_panel, preferred_element_type=jnp.float32)
    mixed_sum = lax.psum_scatter(
        out_terms.astype(jnp.bfloat16), "col", scatter_dimension=1, tiled=True
    ).astype(jnp.float32)
    mixed = (inputs + mixed_sum + down_bias[None, :]).astype(jnp.bfloat16)
    cot_rows = lax.all_gather(cotangent, "col", axis=1, tiled=True)
    hidden_grad = contract_last(cot_rows, down_panel)
    pre_grad = (hidden_grad * gelu_slope(pre_act)).astype(jnp.bfloat16)
    down_term = grad_scale * contract_first(hidden, cot_rows)
    bias_term = grad_scale * jnp.sum(cot_rows, axis=0, dtype=jnp.float32)[None, :]
    down_weight_grad, down_bias_grad = (
        lax.psum_scatter(
            down_term.astype(jnp.bfloat16), "row", scatter_dimension=1, tiled=True
        ).astype(jnp.float32),
        lax.psum_scatter(
            bias_term.astype(jnp.bfloat16), "row", scatter_dimension=1, tiled=True
        ).astype(jnp.float32),
    )
    up_term = grad_scale * contract_first(normed_rows, pre_grad)
    up_weight_grad = lax.psum_scatter(
        up_term.astype(jnp.bfloat16), "row", scatter_dimension=0, tiled=True
    )
    input_terms = contract_last(pre_grad, up_panel)
    normed_grad = lax.psum_scatter(
        input_terms.astype(jnp.bfloat16), "col", scatter_dimension=1, tiled=True
    ).astype(jnp.float32)
    scaled_grad = normed_grad * norm_gain[None, :]
    first_sum, second_sum = lax.psum(
        (jnp.sum(scaled_grad, axis=1), jnp.sum(scaled_grad * normed, axis=1)), "col"
    )
    correction = scaled_grad - first_sum[:, None] / D - normed * (second_sum[:, None] / D)
    patch_grad = (cotangent.astype(jnp.float32) + inv_std * correction).astype(jnp.bfloat16)
    up_bias_grad, gain_grad = lax.psum(
        (
            grad_scale * jnp.sum(pre_grad, axis=0, dtype=jnp.float32),
            grad_scale * jnp.sum(normed_grad * normed, axis=0),
        ),
        "row",
    )
    return (
        mixed,
        patch_grad,
        gain_grad,
        up_weight_grad,
        up_bias_grad,
        down_weight_grad.astype(jnp.bfloat16),
        down_bias_grad[0],
    )


def solution(mesh):
    in_specs = (
        P("row", "col"),
        P("col"),
        P("row", "col"),
        P("col"),
        P("col", "row"),
        P("col"),
        P("row", "col"),
    )
    out_specs = (
        P("row", "col"),
        P("row", "col"),
        P("col"),
        P("row", "col"),
        P("col"),
        P("col", "row"),
        P("row"),
    )
    return jax.shard_map(
        on_device, mesh=mesh, in_specs=in_specs, out_specs=out_specs, check_vma=False
    )
```

profile of v0, /device:TPU:2, one launch (start us, length us, event | category | flops | bytes accessed | tf_op | source)
XLA Modules:
  0.0 602.4 jit_solution(15573838495202693303)
XLA Ops:
  7.9 0.9 convert_reduce_fusion.2
  8.9 29.2 %psum.42 = f32[256]{0:T(256)S(1)} all-reduce(f32[256]{0:T(256)S(1)} %convert_reduce_fusion.2), channel_id=1, replica_groups=mesh['row'=16,'col'=16] {'col'}, use_global_device_ids=true, to_apply=%region_1.0 | all-reduce | flops 256 | bytes 2048 | tf_op jit(solution)/shard_map/psum | solution.py:32
  38.1 0.9 fusion.27
  39.0 23.6 %psum.43 = f32[256]{0:T(256)S(1)} all-reduce(f32[256]{0:T(256)S(1)} %fusion.27), channel_id=1, replica_groups=mesh['row'=16,'col'=16] {'col'}, use_global_device_ids=true, to_apply=%region_3.0 | all-reduce | flops 256 | bytes 2048 | tf_op jit(solution)/shard_map/psum | solution.py:35
  62.7 1.6 fusion.22
  65.7 1.9 convert_reduce_fusion
  67.6 1.3 reshape_bitcast_fusion
  69.0 32.2 %all-gather.5.cloned.1.call-done = bf16[256,3072]{0,1:T(8,128)(2,1)} async-done(((bf16[256,192]{0,1:T(8,128)(2,1)}), bf16[256,3072]{0,1:T(8,128)(2,1)}) %all-gather.5.cloned.1.call-update) | async-done | bytes 1572880 | tf_op jit(solution)/shard_map/all_gather | solution.py:39
  101.3 60.2 %all-gather.7.cloned.1.call-done = bf16[3072,768]{1,0:T(8,128)(2,1)} async-done(((bf16[192,768]{1,0:T(8,128)(2,1)}), bf16[3072,768]{1,0:T(8,128)(2,1)}) %all-gather.7.cloned.1.call-update) | async-done | bytes 4718608 | tf_op jit(solution)/shard_map/all_gather | solution.py:40
  161.5 4.3 convolution_add_fusion
  165.7 56.9 %all-gather.9.cloned.1.call-done = bf16[768,3072]{0,1:T(8,128)(2,1)} async-done(((bf16[768,192]{0,1:T(8,128)(2,1)}), bf16[768,3072]{0,1:T(8,128)(2,1)}) %all-gather.9.cloned.1.call-update) | async-done | bytes 4718608 | tf_op jit(solution)/shard_map/all_gather | solution.py:41
  222.6 4.1 convert_reduce_fusion.1
  226.7 2.6 convolution_convert_fusion
  229.4 6.3 %convolution_convert_fusion.1 = bf16[256,3072]{0,1:T(8,128)(2,1)} fusion(bf16[768,3072]{0,1:T(8,128)(2,1)} %all-gather.9.cloned.1.call-done, f32[256,768]{1,0:T(8,128)S(1)} %convolution_add_fusion), kind=kOutput, calls=%fused_computation.3 | convolution fusion | flops 1221525504 | bytes 7077888 | tf_op jit(solution)/shard_map/dot_general | solution.py:44
  235.7 4.9 multiply_convert_fusion.1
  240.7 5.1 multiply_convert_fusion
  245.8 57.2 %reduce-scatter.16.cloned.1.call-done = bf16[192,1]{1,0:T(8,128)(2,1)} async-done(((bf16[3072,1]{1,0:T(8,128)(2,1)}), bf16[192,1]{1,0:T(8,128)(2,1)}) %reduce-scatter.16.cloned.1.call-update) | async-done | bytes 400
  304.5 59.1 %reduce-scatter.10.cloned.1.call-done = bf16[256,192]{0,1:T(8,128)(2,1)} async-done(((bf16[256,3072]{0,1:T(8,128)(2,1)}), bf16[256,192]{0,1:T(8,128)(2,1)}) %reduce-scatter.10.cloned.1.call-update) | async-done | bytes 98320 | tf_op jit(solution)/shard_map/reduce_scatter | solution.py:67
  363.6 1.0 fusion.29
  364.6 35.4 %all-reduce.1 = (f32[192]{0:T(256)}, f32[768]{0:T(1024)}) all-reduce(f32[192]{0:T(256)S(1)} %broadcast_multiply_fusion.1, f32[768]{0:T(1024)S(1)} %broadcast_multiply_fusion), channel_id=1, replica_groups=mesh['row'=16,'col'=16] {'row'}, use_global_device_ids=true, to_apply=%region_11.0 | all-reduce | flops 960 | bytes 7680 | tf_op jit(solution)/shard_map/psum | solution.py:76
  400.0 23.5 %all-reduce = (f32[256]{0:T(256)S(1)}, f32[256]{0:T(256)S(1)}) all-reduce(f32[256]{0:T(256)S(1)} %get-tuple-element.8, f32[256]{0:T(256)S(1)} %get-tuple-element.9), channel_id=1, replica_groups=mesh['row'=16,'col'=16] {'col'}, use_global_device_ids=true, to_apply=%region_9.0 | all-reduce | flops 512 | bytes 4096 | tf_op jit(solution)/shard_map/psum | solution.py:71
  423.6 1.7 fusion.26
  425.3 83.5 %reduce-scatter.12.cloned.1.call-done = bf16[192,768]{1,0:T(8,128)(2,1)} async-done(((bf16[3072,768]{1,0:T(8,128)(2,1)}), bf16[192,768]{1,0:T(8,128)(2,1)}) %reduce-scatter.12.cloned.1.call-update) | async-done | bytes 294928 | tf_op jit(solution)/shard_map/reduce_scatter | solution.py:63
  508.8 87.1 %reduce-scatter.14.cloned.1.call-done = bf16[768,192]{0,1:T(8,128)(2,1)} async-done(((bf16[768,3072]{0,1:T(8,128)(2,1)}), bf16[768,192]{0,1:T(8,128)(2,1)}) %reduce-scatter.14.cloned.1.call-update) | async-done | bytes 294928 | tf_op jit(solution)/shard_map/reduce_scatter | solution.py:55
  (40 shorter events, 3.9 us)
Async XLA Ops:
  7.2 58.5 %all-gather.11.cloned.1.call-start = ((), (), s32[]{:S(2)}) async-start(), calls=%async_computation.9 | async-start | bytes 1671168 | tf_op jit(solution)/shard_map/all_gather | solution.py:49
  7.9 93.4 %all-gather.5.cloned.1.call-start = ((), (), s32[]{:S(2)}) async-start(), calls=%async_computation.5 | async-start | bytes 1671168 | tf_op jit(solution)/shard_map/all_gather | solution.py:39
  64.3 97.2 %all-gather.7.cloned.1.call-start = ((), (), s32[]{:S(2)}) async-start(), calls=%async_computation.6 | async-start | bytes 5013504 | tf_op jit(solution)/shard_map/all_gather | solution.py:40
  65.1 157.6 %all-gather.9.cloned.1.call-start = ((), (), s32[]{:S(2)}) async-start(), calls=%async_computation.7 | async-start | bytes 5013504 | tf_op jit(solution)/shard_map/all_gather | solution.py:41
  65.6 237.4 %reduce-scatter.16.cloned.1.call-start = ((), (), s32[]{:S(2)}) async-start(), calls=%async_computation.13 | async-start | bytes 835584
  69.0 153.7 %copy-start = (bf16[256,3072]{0,1:T(8,128)(2,1)S(1)}, bf16[256,3072]{0,1:T(8,128)(2,1)}, u32[]{:S(2)}) copy-start(bf16[256,3072]{0,1:T(8,128)(2,1)} %all-gather.11.cloned.1.call-done) | copy-start | bytes 4718596
  69.0 294.6 %reduce-scatter.10.cloned.1.call-start = ((), (), s32[]{:S(2)}) async-start(), calls=%async_computation.10 | async-start | bytes 1671168 | tf_op jit(solution)/shard_map/reduce_scatter | solution.py:67
  222.6 4.1 copy-start.5
  229.3 194.2 %reduce-scatter.8.cloned.1.call-start = ((), (), s32[]{:S(2)}) async-start(), calls=%async_computation.8 | async-start | bytes 1671168 | tf_op jit(solution)/shard_map/reduce_scatter | solution.py:45
  235.7 273.1 %reduce-scatter.12.cloned.1.call-start = ((), (), s32[]{:S(2)}) async-start(), calls=%async_computation.11 | async-start | bytes 5013504 | tf_op jit(solution)/shard_map/reduce_scatter | solution.py:63
  240.7 355.2 %reduce-scatter.14.cloned.1.call-start = ((), (), s32[]{:S(2)}) async-start(), calls=%async_computation.12 | async-start | bytes 5013504 | tf_op jit(solution)/shard_map/reduce_scatter | solution.py:55
  245.8 117.8 %copy-start.1 = (bf16[256,192]{0,1:T(8,128)(2,1)S(1)}, bf16[256,192]{0,1:T(8,128)(2,1)}, u32[]{:S(2)}) copy-start(bf16[256,192]{0,1:T(8,128)(2,1)} %param.7) | copy-start | bytes 294916
  245.8 117.8 %copy-start.3 = (f32[192]{0:T(256)S(1)}, f32[192]{0:T(256)}, u32[]{:S(2)}) copy-start(f32[192]{0:T(256)} %param.8) | copy-start | bytes 2308
  245.8 177.7 %copy-start.2 = (bf16[256,192]{0,1:T(8,128)(2,1)S(1)}, bf16[256,192]{0,1:T(8,128)(2,1)}, u32[]{:S(2)}) copy-start(bf16[256,192]{0,1:T(8,128)(2,1)} %param.13) | copy-start | bytes 294916
  245.8 177.8 %copy-start.4 = (f32[192]{0:T(256)S(1)}, f32[192]{0:T(256)}, u32[]{:S(2)}) copy-start(f32[192]{0:T(256)} %param.12) | copy-start | bytes 2308
Sparse Core Ops, SparseCore 0:
  9.8 41.9 all-gather.10
  64.4 36.7 all-gather.4
  103.8 57.6 all-gather.6
  163.8 58.7 all-gather.8
  225.9 77.0 reduce-scatter.15
  305.4 58.0 reduce-scatter.9
  366.3 56.8 reduce-scatter.7
  427.3 81.3 reduce-scatter.11
  513.0 82.8 reduce-scatter.13
where the time goes:
time: 603 us; the launch traced here: 602 us
  waiting for transfers between devices  438 us (73%)
  blocking collectives  112 us (19%)
  matrix products  27.2 us (5%)
  between operations  13.9 us (2%)
  other arithmetic  9.03 us (1%)
    reduce_scatter x1, waiting for transfers between devices, on_device(): lax.psum_scatter(down_term.astype(jnp.bfloat16), 'row', scatter_dimension...  87.1 us
    reduce_scatter x1, waiting for transfers between devices, on_device(): lax.psum_scatter(up_term.astype(jnp.bfloat16), 'row', scatter_dimension=0...  83.5 us
    all_gather x1, waiting for transfers between devices, on_device(): up_panel = lax.all_gather(up_weight, 'row', axis=0, tiled=True)  60.2 us
    unnamed x10, waiting for transfers between devices  59.2 us
    reduce_scatter x1, waiting for transfers between devices, on_device(): lax.psum_scatter(input_terms.astype(jnp.bfloat16), 'col', scatter_dimensi...  59.1 us
    all_gather x1, waiting for transfers between devices, on_device(): down_panel = lax.all_gather(down_weight, 'row', axis=1, tiled=True)  56.9 us
    psum x1, blocking collectives, on_device(): lax.psum((grad_scale * jnp.sum(pre_grad, axis=0, dtype=jnp.float32), grad...  35.4 us
    all_gather x1, waiting for transfers between devices, on_device(): normed_rows = lax.all_gather(normed_bf, 'col', axis=1, tiled=True)  32.2 us
  transfers between devices with their start and end apart: 9, of which 7 were waited for; matrix products, arithmetic and copies ran while one was open for 6% of the time, Pallas kernels for 0%

commit v1 on v0

v1 whole, which is shorter than its diff:
```python
import functools
import math

import jax
import jax.numpy as jnp
from jax import lax
from jax.experimental import pallas as pl
from jax.experimental.pallas import tpu as pltpu
from jax.sharding import PartitionSpec as P

MESH = pl.DeviceIdType.MESH
BF = jnp.bfloat16
F32 = jnp.float32

NB = 16
FB = 192
TB = 256
HB = 384
D = NB * FB
N_SEM = 320


def rem(a, n):
    return lax.rem(a, n)


def tn_dot(left, right):
    return lax.dot_general(
        left, right, (((0,), (0,)), ((), ())), preferred_element_type=F32
    )


def nn_dot(left, right):
    return jnp.dot(left, right, preferred_element_type=F32)


def kernel(
    scale,
    patches, gain, w1in, ubias, w2in, dbias, cot,
    mixed_o, pgrad_o, gaing_o, dw1_o, ubg_o, dw2_o, dbg_o,
    XT, XN, CT, W1, W2, W1H, W2H,
    GA, UB, BC, GW, MI,
    PRE, SL, HG, HID, PG, HIDR, PGR,
    MX, MXS, MXP, MXM, MXT,
    NG, NGS, NGP, NGM, NGT,
    G1, G1Y, G1X, G1T, G1F,
    G2, G2Y, G2X, G2T, G2F,
    ST, STS, STZ, STT,
    MS, RM, UT, FU, GT, GTX, GTY,
    ss, rs,
):
    r = lax.axis_index("row")
    c = lax.axis_index("col")
    x, y = r // 4, rem(r, 4)
    z, k = c // 2, rem(c, 2)
    g = y // 2
    yh = y + 1 - 2 * rem(y, 2)
    yt = 3 - y
    own = g == k
    other = g != k

    def dev(xx, yy, zz, kk):
        return (xx * 4 + yy, zz * 2 + kk)

    def zdev(j):
        return dev(x, y, rem(z + j + 8, 8), k)

    def xdev(j):
        return dev(rem(x + j + 4, 4), y, z, k)

    sib = dev(x, y, z, 1 - k)
    hdev = dev(x, yh, z, k)
    tdev = dev(x, yt, z, k)
    tdev2 = dev(x, yt, z, 1 - k)

    def zb(j, kk):
        return rem(z + j + 8, 8) * 2 + kk

    def wb(j, yy):
        return rem(x + j + 4, 4) * 4 + yy

    b0 = zb(0, k)

    ids = {}
    made = {}

    def sem(name):
        return ids.setdefault(name, len(ids))

    def rc(sname, rname, src, dst, to):
        return pltpu.make_async_remote_copy(
            src_ref=src, dst_ref=dst, send_sem=ss.at[sem(sname)], recv_sem=rs.at[sem(rname)],
            device_id=to, device_id_type=MESH,
        )

    def send(name, src, dst, to):
        copy = rc(name, name, src, dst, to)
        copy.start()
        made[name] = copy

    def got(*names):
        for name in names:
            made[name].wait_recv()

    barrier = pltpu.get_barrier_semaphore()
    peers = [zdev(j) for j in range(1, 8)] + [xdev(j) for j in range(1, 4)]
    peers += [dev(x, rem(y + j, 4), z, k) for j in range(1, 4)]
    peers += [dev(rem(x + j, 4), yh, z, k) for j in range(1, 4)]
    peers += [sib, tdev2]
    for peer in peers:
        pl.semaphore_signal(barrier, inc=1, device_id=peer, device_id_type=MESH)

    XT[0, b0] = patches[...].T
    W1H[0] = w1in[:, :HB]
    W1H[1] = w1in[:, HB:]
    GA[k, z] = jnp.zeros((8, 256), F32)
    GA[k, z, :, 0:FB] = jnp.broadcast_to(gain[...], (8, FB))
    UB[0] = jnp.broadcast_to(ubias[:, pl.ds(pl.multiple_of(k * HB, 128), HB)], (8, HB))
    UB[1] = jnp.broadcast_to(ubias[:, pl.ds(pl.multiple_of((1 - k) * HB, 128), HB)], (8, HB))
    pl.semaphore_wait(barrier, len(peers))

    def tok_edge(t, A):
        send(t + "T", A.at[0, b0], A.at[1, b0], tdev)

    def tok_first(t, A, s):
        send(f"{t}p1{s}", A.at[s, b0], A.at[s, b0], zdev(1))
        send(f"{t}m1{s}", A.at[s, b0], A.at[s, b0], zdev(-1))
        send(f"{t}sib0{s}", A.at[s, b0], A.at[s, b0], sib)

    def tok_next(t, A, s, n):
        bp, bm = zb(-n, k), zb(n, k)
        got(f"{t}p{n}{s}")
        if n < 3:
            send(f"{t}p{n + 1}{s}", A.at[s, bp], A.at[s, bp], zdev(1))
        else:
            half = pl.ds(0, FB // 2)
            send(f"{t}p4{s}", A.at[s, bp, half], A.at[s, bp, half], zdev(1))
        got(f"{t}m{n}{s}")
        if n < 3:
            send(f"{t}m{n + 1}{s}", A.at[s, bm], A.at[s, bm], zdev(-1))
        else:
            half = pl.ds(FB // 2, FB // 2)
            send(f"{t}m4{s}", A.at[s, bm, half], A.at[s, bm, half], zdev(-1))
        send(f"{t}sibp{n}{s}", A.at[s, bp], A.at[s, bp], sib)
        send(f"{t}sibm{n}{s}", A.at[s, bm], A.at[s, bm], sib)

    def tok_last(t, A, s):
        b4 = zb(4, k)
        got(f"{t}p4{s}", f"{t}m4{s}")
        send(f"{t}sib4{s}", A.at[s, b4], A.at[s, b4], sib)

    def tok_done(t, s):
        for n in ("0", "p1", "m1", "p2", "m2", "p3", "m3", "4"):
            got(f"{t}sib{n}{s}")

    r0, rt = wb(0, y), wb(0, yt)

    def w_start(t, WH, W):
        @pl.when(own)
        def _():
            W[r] = WH[k]
            rc(t + "b", t + "u0", WH.at[1 - k], W.at[r], sib).start()

        @pl.when(other)
        def _():
            rc(t + "a", t + "u1", WH.at[k], W.at[r], tdev).start()
            rc(t + "b", t + "u1", WH.at[1 - k], W.at[r], tdev2).start()

    def w_u0(t, WH, W):
        @pl.when(other)
        def _():
            rc(t + "b", t + "u0", WH.at[1 - k], W.at[r], sib).wait_recv()

        send(t + "P+", W.at[r0], W.at[r0], xdev(1))
        send(t + "P-", W.at[r0], W.at[r0], xdev(-1))
        send(t + "Y0", W.at[r0], W.at[r0], hdev)

    def w_u1(t, WH, W):
        rc(t + "a", t + "u1", WH.at[k], W.at[rt], tdev).wait_recv()
        send(t + "Q0", W.at[rt], W.at[rt], hdev)
        send(t + "Q+", W.at[rt], W.at[rt], xdev(1))
        send(t + "Q-", W.at[rt], W.at[rt], xdev(-1))

    lo, hi = pl.ds(0, FB // 2), pl.ds(FB // 2, FB // 2)

    def w_half(t, n, W, yy, relay):
        bp, bm = wb(-1, yy), wb(1, yy)
        got(f"{t}{n}+")
        send(f"{t}{n}2+", W.at[bp, lo], W.at[bp, lo], xdev(1))
        got(f"{t}{n}-")
        send(f"{t}{n}2-", W.at[bm, hi], W.at[bm, hi], xdev(-1))
        if relay:
            send(t + "Y1", W.at[bp], W.at[bp], hdev)
            send(t + "Y2", W.at[bm], W.at[bm], hdev)

    def w_p1(t, W):
        w_half(t, "P", W, y, True)

    def w_q0(t, W):
        b = wb(0, 3 - yh)
        got(t + "Q0")
        send(t + "R+", W.at[b], W.at[b], xdev(1))
        send(t + "R-", W.at[b], W.at[b], xdev(-1))

    def w_q1(t, W):
        w_half(t, "Q", W, yt, False)

    def w_r1(t, W):
        w_half(t, "R", W, 3 - yh, False)

    def w_p2(t, W):
        b = wb(2, y)
        got(t + "P2+", t + "P2-")
        send(t + "Y3", W.at[b], W.at[b], hdev)

    def w_done(t):
        got(*(t + n for n in ("Q2+", "Q2-", "R2+", "R2-", "Y0", "Y1", "Y2", "Y3")))

    tok_edge("X", XT)
    tok_first("X", XT, 0)
    w_start("V", W1H, W1)
    CT[0, b0] = cot[...].T
    W2H[0] = w2in[:HB].T
    W2H[1] = w2in[HB:].T
    send("ub", UB.at[1], UB.at[2], sib)
    for j in range(1, 8):
        send(f"ga{j}", GA.at[k, z], GA.at[k, z], zdev(j))
    w_u0("V", W1H, W1)
    got("XT")
    tok_first("X", XT, 1)
    tok_edge("C", CT)
    w_start("U", W2H, W2)
    tok_next("X", XT, 0, 1)
    w_u1("V", W1H, W1)
    w_p1("V", W1)
    tok_next("X", XT, 1, 1)
    tok_first("C", CT, 0)
    tok_next("X", XT, 0, 2)
    w_q0("V", W1)
    w_q1("V", W1)
    w_u0("U", W2H, W2)
    tok_next("X", XT, 1, 2)
    tok_next("X", XT, 0, 3)
    got("CT")
    tok_first("C", CT, 1)
    w_u1("U", W2H, W2)
    w_p2("V", W1)
    tok_next("X", XT, 1, 3)
    w_r1("V", W1)
    tok_next("C", CT, 0, 1)
    tok_last("X", XT, 0)
    w_p1("U", W2)
    tok_next("C", CT, 1, 1)
    tok_last("X", XT, 1)
    for j in range(1, 8):
        got(f"ga{j}")
    send("gas", GA.at[k], GA.at[k], sib)
    w_q0("U", W2)
    w_q1("U", W2)

    def blocks_sum(slot, term):
        def step(b, total):
            return total + term(XT[slot, b].astype(F32)).reshape(FB // 8, 8, TB).sum(0)

        total = lax.fori_loop(0, NB, step, jnp.zeros((8, TB), F32))
        return jnp.sum(total, axis=0, keepdims=True)

    def statistics(slot):
        mean = blocks_sum(slot, lambda v: v) / D
        var = blocks_sum(slot, lambda v: (v - mean) * (v - mean)) / D
        MI[slot, 0:1] = mean
        MI[slot, 1:2] = lax.rsqrt(var + 1e-06)

    tok_done("X", 0)
    statistics(0)
    tok_next("C", CT, 0, 2)
    w_p2("U", W2)
    tok_done("X", 1)
    statistics(1)
    tok_next("C", CT, 1, 2)
    w_r1("U", W2)
    got("gas", "ub")

    def gain_column(kk, zz):
        return GA[kk, zz].T[:FB, 0:1]

    def normalise(b, gw):
        column = gain_column(rem(b, 2), b // 2)
        for slot in range(2):
            v = (XT[slot, b].astype(F32) - MI[slot, 0:1]) * MI[slot, 1:2]
            XN[slot, b] = (v * column).astype(BF)
        return gw

    lax.fori_loop(0, NB // 2, normalise, 0)
    tok_next("C", CT, 0, 3)
    lax.fori_loop(NB // 2, NB, normalise, 0)
    tok_next("C", CT, 1, 3)
    tok_last("C", CT, 0)

    w_done("V")
    GRP = 4

    def panel_dot(W, A, out):
        for j in range(NB // GRP):
            wt = W[j * GRP:(j + 1) * GRP].reshape(GRP * FB, HB).T
            for slot in range(2):
                part = nn_dot(wt, A[slot, j * GRP:(j + 1) * GRP].reshape(GRP * FB, TB))
                if j == 0:
                    out[slot] = part
                else:
                    out[slot] += part

    panel_dot(W1, XN, PRE)
    tok_last("C", CT, 1)
    bias = jnp.where(own, UB[0], UB[2])
    BC[...] = jnp.broadcast_to(bias.T[:, 0:1], (HB, 128))

    CH = 64

    def gelu_rows(i, carry):
        rows = pl.ds(pl.multiple_of(i * CH, CH), CH)
        for slot in range(2):
            v = PRE[slot, rows] + BC[rows, 0:1]
            cdf = 0.5 * (1.0 + lax.erf(v * 0.7071067811865476))
            HID[slot, rows] = (v * cdf).astype(BF)
            SL[slot, rows] = cdf + v * jnp.exp(-0.5 * v * v) * 0.3989422804014327
        return carry

    lax.fori_loop(0, HB // CH, gelu_rows, 0)
    for slot in range(2):
        HIDR[slot] = HID[slot].T

    def z_make(t, W, A, M, S, j):
        pair = rem(z + j + 8, 8)
        w = W[pl.ds(pl.multiple_of(pair * 2, 2), 2)].reshape(2 * FB, HB)
        for slot in range(2):
            part = nn_dot(w, A[slot]).astype(BF)
            M[slot, pair * 2] = part[:FB]
            M[slot, pair * 2 + 1] = part[FB:]
        send(f"{t}s{j}", M.at[:, pair * 2 + 1 - k], S.at[j + 3], sib)

    def z_send(t, M, S, RP, RN, j):
        b = zb(j, k)
        got(f"{t}s{j}")
        for slot in (1, 0):
            total = M[slot, b].astype(F32) + S[j + 3, slot].astype(F32)
            if j == 3 and slot == 0 or j in (1, 2):
                got(f"{t}+{j + 1}{slot}")
                total = total + RP[slot, 3 - j].astype(F32)
            if j == -3 and slot == 1 or j in (-1, -2):
                got(f"{t}-{1 - j}{slot}")
                total = total + RN[slot, 3 + j].astype(F32)
            M[slot, b] = total.astype(BF)
            if j == 4:
                if slot == 0:
                    send(f"{t}+4{slot}", M.at[slot, b], RP.at[slot, 0], zdev(1))
                else:
                    send(f"{t}-4{slot}", M.at[slot, b], RN.at[slot, 0], zdev(-1))
            elif j > 0:
                send(f"{t}+{j}{slot}", M.at[slot, b], RP.at[slot, 4 - j], zdev(1))
            else:
                send(f"{t}-{-j}{slot}", M.at[slot, b], RN.at[slot, 4 + j], zdev(-1))

    def z_total(t, M, S, RP, RN, slot):
        got(f"{t}+1{slot}", f"{t}-1{slot}")
        total = M[slot, b0].astype(F32) + S[3, slot].astype(F32)
        return total + RP[slot, 3].astype(F32) + RN[slot, 3].astype(F32)

    def z_edge(t, M, S, RP, RN, RT):
        got(f"{t}s0")
        M[1, b0] = z_total(t, M, S, RP, RN, 1).astype(BF)
        send(t + "T", M.at[1, b0], RT, tdev)

    def z_final(t, M, S, RP, RN, RT):
        total = z_total(t, M, S, RP, RN, 0)
        got(t + "T")
        return total + RT[...].astype(F32)

    ORDER = (4, 3, -3, 2, -2, 1, -1, 0)
    ma = ("M", MX, MXS, MXP, MXM)
    na = ("N", NG, NGS, NGP, NGM)

    w_done("U")
    for j in ORDER[:3]:
        z_make("M", W2, HID, MX, MXS, j)
    z_send(*ma, 4)
    for j in ORDER[3:]:
        z_make("M", W2, HID, MX, MXS, j)
    tok_done("C", 0)
    tok_done("C", 1)

    yq = 3 - yh

    def g_make(A, B, G, blocks):
        for b in blocks:
            part = nn_dot(A[0, b], B[0]) + nn_dot(A[1, b], B[1])
            G[b] = (part * scale).astype(BF)

    def g_hid(t, G, RY):
        for j in (2, 1, -1, 0):
            b = wb(j, yh)
            send(f"{t}h{j}", G.at[b], RY.at[j + 1], hdev)

    def g_far(t, G, RX, n, yy):
        b = wb(2, yy)
        send(f"{t}{n}2+", G.at[b, lo], RX.at[0, lo], xdev(1))
        send(f"{t}{n}2-", G.at[b, hi], RX.at[0, hi], xdev(-1))

    def g_near(t, G, RX, n, yy):
        for j, tail, rows in ((1, "+", lo), (-1, "-", hi)):
            b = wb(j, yy)
            got(f"{t}{n}2{tail}")
            G[b, rows] = (G[b, rows].astype(F32) + RX[0, rows].astype(F32)).astype(BF)
            send(f"{t}{n}1{tail}", G.at[b], RX.at[1 if j > 0 else 2], xdev(j))

    def g_total(t, G, RX, n, yy):
        got(f"{t}{n}1+", f"{t}{n}1-")
        total = G[wb(0, yy)].astype(F32) + RX[1].astype(F32)
        return total + RX[2].astype(F32)

    def g_add(t, G, RY, j):
        b = wb(j, y)
        got(f"{t}h{j}")
        G[b] = (G[b].astype(F32) + RY[j + 1].astype(F32)).astype(BF)

    def g_step0(t, G, RY, RX):
        g_far(t, G, RX.at[1], "w", yq)
        g_far(t, G, RX.at[2], "t", yt)

    def g_step1(t, G, RY, RX):
        g_add(t, G, RY, 2)
        g_far(t, G, RX.at[0], "o", y)

    def g_step2(t, G, RY, RX):
        g_near(t, G, RX.at[1], "w", yq)
        g_near(t, G, RX.at[2], "t", yt)

    def g_step3(t, G, RY, RX):
        g_add(t, G, RY, 1)
        g_add(t, G, RY, -1)
        g_near(t, G, RX.at[0], "o", y)
        g_add(t, G, RY, 0)

    def g_step4(t, G, RY, RX, T):
        T[0] = g_total(t, G, RX.at[1], "w", yq).astype(BF)
        send(t + "w", T.at[0], RY.at[4], hdev)

    def g_step5(t, G, RY, RX, T, out):
        T[1] = g_total(t, G, RX.at[0], "o", y).astype(BF)
        got(t + "w")
        T[2] = (g_total(t, G, RX.at[2], "t", yt) + RY[4].astype(F32)).astype(BF)
        deliver(t, T.at[1], T.at[2], out)

    def deliver(t, T0, T1, out):
        @pl.when(own)
        def _():
            out[k] = T0[...]
            rc(t + "f1", t + "q1", T1, out.at[k], tdev).start()

        @pl.when(other)
        def _():
            rc(t + "f0", t + "q0", T0, out.at[k], sib).start()
            rc(t + "f1", t + "q2", T1, out.at[k], tdev2).start()

    def finish(t, T0, T1, out):
        @pl.when(own)
        def _():
            rc(t + "f0", t + "q0", T0, out.at[1 - k], sib).wait_recv()

        @pl.when(other)
        def _():
            rc(t + "f1", t + "q1", T1, out.at[k], tdev).wait_recv()
            rc(t + "f1", t + "q2", T1, out.at[1 - k], tdev2).wait_recv()

    def delivered(t, T0, T1, out):
        rc(t + "f1", t + "q1", T1, out.at[k], tdev).wait_send()

        @pl.when(other)
        def _():
            rc(t + "f0", t + "q0", T0, out.at[k], sib).wait_send()

    d2 = ("D", G2, G2Y, G2X)
    d1 = ("E", G1, G1Y, G1X)

    def g_blocks(yy, js=(0, 1, 2, 3)):
        return [wb(j, yy) for j in js]

    g_make(CT, HIDR, G2, g_blocks(yh))
    g_hid("D", G2, G2Y)
    g_make(CT, HIDR, G2, [wb(2, yq), wb(2, yt)])
    g_step0(*d2)
    z_send(*ma, 3)
    z_send(*ma, -3)
    g_make(CT, HIDR, G2, [wb(2, y), wb(1, yq), wb(-1, yq), wb(1, yt), wb(-1, yt)])
    g_step1(*d2)
    panel_dot(W2, CT, HG)
    g_step2(*d2)
    z_send(*ma, 2)
    z_send(*ma, -2)
    g_make(CT, HIDR, G2, [wb(1, y), wb(-1, y), wb(0, yq), wb(0, yt), wb(0, y)])

    def gain_weight(b, total):
        column = gain_column(rem(b, 2), b // 2)
        return total + (W1[b].astype(F32) * column).reshape(FB // 8, 8, HB).sum(0)

    gw = lax.fori_loop(0, NB, gain_weight, jnp.zeros((8, HB), F32))
    gw = jnp.broadcast_to(jnp.sum(gw, axis=0, keepdims=True), (8, HB))
    GW[...] = jnp.broadcast_to(gw.T[:, 0:1], (HB, 128))

    def slope_rows(slot, i, sums):
        first, second = sums
        rows = pl.ds(pl.multiple_of(i * CH, CH), CH)
        grad = (HG[slot, rows] * SL[slot, rows]).astype(BF)
        PG[slot, rows] = grad
        wide = grad.astype(F32)
        first += (wide * GW[rows, 0:1]).reshape(CH // 8, 8, TB).sum(0)
        second += (wide * PRE[slot, rows]).reshape(CH // 8, 8, TB).sum(0)
        return first, second

    zero = jnp.zeros((8, TB), F32)
    line = lax.broadcasted_iota(jnp.int32, (8, TB), 0)
    up_sum = jnp.zeros((1, HB), F32)
    for slot in range(2):
        first, second = lax.fori_loop(0, HB // CH, functools.partial(slope_rows, slot), (zero, zero))
        first = jnp.sum(first, axis=0, keepdims=True)
        second = jnp.sum(second, axis=0, keepdims=True)
        ST[0, slot] = jnp.where(line == 0, first, jnp.where(line == 1, second, 0.0))
        turned = PG[slot].T
        PGR[slot] = turned
        up_sum += jnp.sum(turned.astype(F32), axis=0, keepdims=True)
    send("st", ST.at[0], STS, sib)

    g_make(XN, PGR, G1, g_blocks(yh))
    g_hid("E", G1, G1Y)
    g_make(XN, PGR, G1, [wb(2, yq), wb(2, yt)])
    g_step0(*d1)
    z_make("N", W1, PG, NG, NGS, 4)
    z_send(*ma, 1)
    z_send(*ma, -1)
    g_step3(*d2)
    z_send(*na, 4)
    z_make("N", W1, PG, NG, NGS, 3)
    z_make("N", W1, PG, NG, NGS, -3)
    g_make(XN, PGR, G1, [wb(2, y), wb(1, yq), wb(-1, yq), wb(1, yt), wb(-1, yt)])
    g_step4(*d2, G2T)
    g_step1(*d1)
    for j in ORDER[3:]:
        z_make("N", W1, PG, NG, NGS, j)

    peers8 = [(j, h) for j in range(4) for h in range(2)]

    def bias_row(b):
        v = CT[0, b].astype(F32) + CT[1, b].astype(F32)
        return jnp.sum((v[:, :128] + v[:, 128:]).T, axis=0, keepdims=True)

    for i, (j, h) in enumerate(peers8):
        yy = yh if h else y
        MS[i, :, 0:HB] = jnp.broadcast_to(up_sum, (8, HB))
        MS[i, :, HB:HB + 128] = jnp.zeros((8, 128), F32)
        MS[i, :, HB + 128:] = jnp.zeros((8, 128), F32)
        MS[i, :, HB:HB + FB] = jnp.broadcast_to(bias_row(wb(j, yy)), (8, FB))
        if i:
            send(f"ms{i}", MS.at[i], RM.at[i], dev(rem(x + j, 4), yy, z, k))
    got("st")
    ST[1] = ST[0] + STS[...]
    for j in range(1, 8):
        send(f"st{j}", ST.at[1], STZ.at[j], zdev(j))

    g_make(XN, PGR, G1, [wb(1, y), wb(-1, y), wb(0, yq), wb(0, yt), wb(0, y)])
    z_send(*na, 3)
    z_send(*na, -3)
    g_step2(*d1)
    z_edge(*ma, MXT)
    g_step5(*d2, G2T, G2F)

    total = MS[0]
    for i in range(1, 8):
        got(f"ms{i}")
        total = total + RM[i]
    UT[...] = total[:, :HB]
    dbg_o[...] = total[0:1, HB:HB + FB] * scale
    deliver("B", UT, UT, FU)
    total = ST[1]
    for j in range(1, 8):
        got(f"st{j}")
        total = total + STZ[j]
    ST[2] = total
    send("stt", ST.at[2, 1], STT, tdev)

    z_send(*na, 2)
    z_send(*na, -2)
    mixed = z_final(*ma, MXT).T
    mixed_o[...] = (patches[...].astype(F32) + mixed + dbias[...]).astype(BF)
    g_step3(*d1)
    finish("D", G2T.at[1], G2T.at[2], G2F)
    dw2_o[:HB] = G2F[0].T
    dw2_o[HB:] = G2F[1].T
    finish("B", UT, UT, FU)
    ubg_o[:, :HB] = FU[0, 0:1] * scale
    ubg_o[:, HB:] = FU[1, 0:1] * scale
    z_send(*na, 1)
    z_send(*na, -1)
    g_step4(*d1, G1T)

    got("stt")
    sums = ST[2, 0] + STT[...]
    first = sums[0:1] / D
    second = sums[1:2] / D
    column = gain_column(k, z)
    inv_std = MI[0, 1:2]
    normed = (XT[0, b0].astype(F32) - MI[0, 0:1]) * inv_std

    z_edge(*na, NGT)
    g_step5(*d1, G1T, G1F)
    grad = z_final(*na, NGT)
    product = jnp.sum((grad * normed).T, axis=0, keepdims=True)
    GT[0] = jnp.zeros((8, 256), F32)
    GT[0, :, 0:FB] = jnp.broadcast_to(product, (8, FB))
    for j in range(1, 4):
        send(f"gx{j}", GT.at[0], GTX.at[j], xdev(j))
    correction = grad * column - first - normed * second
    result = CT[0, b0].astype(F32) + inv_std * correction
    pgrad_o[...] = result.T.astype(BF)
    total = GT[0]
    for j in range(1, 4):
        got(f"gx{j}")
        total = total + GTX[j]
    GT[1] = total
    for j in range(1, 4):
        send(f"gy{j}", GT.at[1], GTY.at[j], dev(x, rem(y + j, 4), z, k))
    finish("E", G1T.at[1], G1T.at[2], G1F)
    dw1_o[:, :HB] = G1F[0]
    dw1_o[:, HB:] = G1F[1]
    for j in range(1, 4):
        got(f"gy{j}")
        total = total + GTY[j]
    gaing_o[...] = total[0:1, :FB] * scale

    for copy in made.values():
        copy.wait_send()
    for t, WH, W in (("V", W1H, W1), ("U", W2H, W2)):
        rc(t + "b", t + "u0", WH.at[1 - k], W.at[r], sib).wait_send()

        @pl.when(other)
        def _(t=t, WH=WH, W=W):
            rc(t + "a", t + "u1", WH.at[k], W.at[r], tdev).wait_send()

    delivered("D", G2T.at[1], G2T.at[2], G2F)
    delivered("E", G1T.at[1], G1T.at[2], G1F)
    delivered("B", UT, UT, FU)
    assert len(ids) <= N_SEM


def on_device(patches, norm_gain, up_weight, up_bias, down_weight, down_bias, cotangent):
    scale = 1.0 / math.sqrt(patches.shape[0] * lax.axis_size("row"))
    vm = pltpu.VMEM
    tokens = vm((2, NB, FB, TB), BF)
    panel = vm((NB, FB, HB), BF)
    tile = vm((2, HB, TB), F32)
    ring = vm((2, 4, FB, TB), BF)
    scatter_z = [tokens, vm((8, 2, FB, TB), BF), ring, ring, vm((FB, TB), BF)]
    scatter_w = [panel, vm((5, FB, HB), BF), vm((3, 3, FB, HB), BF), vm((3, FB, HB), BF), vm((2, FB, HB), BF)]
    scratch = [
        tokens, tokens, tokens, panel, panel, vm((2, FB, HB), BF), vm((2, FB, HB), BF),
        vm((2, 8, 8, 256), F32), vm((3, 8, HB), F32), vm((HB, 128), F32), vm((HB, 128), F32), vm((2, 8, TB), F32),
        tile, tile, tile, vm((2, HB, TB), BF), vm((2, HB, TB), BF), vm((2, TB, HB), BF), vm((2, TB, HB), BF),
        *scatter_z, *scatter_z, *scatter_w, *scatter_w,
        vm((3, 2, 8, TB), F32), vm((2, 8, TB), F32), vm((8, 2, 8, TB), F32), vm((8, TB), F32),
        vm((8, 8, HB + 256), F32), vm((8, 8, HB + 256), F32), vm((8, HB), F32), vm((2, 8, HB), F32),
        vm((2, 8, 256), F32), vm((4, 8, 256), F32), vm((4, 8, 256), F32),
        pltpu.SemaphoreType.DMA((N_SEM,)), pltpu.SemaphoreType.DMA((N_SEM,)),
    ]
    shape = jax.ShapeDtypeStruct
    whole = pl.BlockSpec(memory_space=pltpu.VMEM)
    mixed, patch_grad, gain_grad, up_grad, up_bias_grad, down_grad, down_bias_grad = pl.pallas_call(
        functools.partial(kernel, scale),
        out_shape=(
            shape((TB, FB), BF), shape((TB, FB), BF), shape((1, FB), F32), shape((FB, 2 * HB), BF),
            shape((1, 2 * HB), F32), shape((2 * HB, FB), BF), shape((1, FB), F32),
        ),
        in_specs=[whole] * 7,
        out_specs=(whole,) * 7,
        scratch_shapes=scratch,
        compiler_params=pltpu.CompilerParams(
            collective_id=0, has_side_effects=True, vmem_limit_bytes=60 << 20
        ),
        name="mlp_block",
    )(patches, norm_gain[None, :], up_weight, up_bias[None, :], down_weight, down_bias[None, :], cotangent)
    return (
        mixed, patch_grad, gain_grad[0], up_grad, up_bias_grad[0], down_grad, down_bias_grad[0],
    )


def solution(mesh):
    in_specs = (
        P("row", "col"),
        P("col"),
        P("row", "col"),
        P("col"),
        P("col", "row"),
        P("col"),
        P("row", "col"),
    )
    out_specs = (
        P("row", "col"),
        P("row", "col"),
        P("col"),
        P("row", "col"),
        P("col"),
        P("col", "row"),
        P("row"),
    )
    return jax.shard_map(
        on_device, mesh=mesh, in_specs=in_specs, out_specs=out_specs, check_vma=False
    )
```

time: 603 us -> 129 us (0.21)
  waiting for transfers between devices: 438 us -> 0 us
  Pallas kernels: 0 us -> 115 us
  blocking collectives: 112 us -> 0 us
  matrix products: 27.2 us -> 0 us
  between operations: 13.9 us -> 0.67 us
  local copies, waits for them, and re-layouts: 2.01 us -> 11.6 us
  other arithmetic: 9.03 us -> 1.29 us
    reduce_scatter x4 -> x0, waiting for transfers between devices: 230 us -> none  [the longest x1 87.1 us: on_device(): lax.psum_scatter(down_term.astype(jnp.bfloat16), 'row', scatter_dimension...]
    all_gather x4 -> x0, waiting for transfers between devices: 149 us -> none  [the longest x1 60.2 us: on_device(): up_panel = lax.all_gather(up_weight, 'row', axis=0, tiled=True)]
    pallas_call x0 -> x1, Pallas kernels: none -> 115 us  [on_device(): pl.pallas_call(functools.partial(kernel, scale), out_shape=(shape((TB, FB...]
    psum x4 -> x0, blocking collectives: 112 us -> none  [the longest x1 35.4 us: on_device(): lax.psum((grad_scale * jnp.sum(pre_grad, axis=0, dtype=jnp.float32), grad...]
    unnamed x10 -> x0, waiting for transfers between devices: 59.2 us -> none
    dot_general x6 -> x0, matrix products: 27.2 us -> none  [the longest x2 9.99 us: contract_first(): lax.dot_general(left, right, (((0,), (0,)), ((), ())), preferred_element_...]
    unnamed x14 -> x19, local copies, waits for them, and re-layouts: 2.01 us -> 10.3 us
  transfers between devices with their start and end apart: 9 -> 0, of which waited for: 7 -> 0; matrix products, arithmetic and copies ran while one was open for 6% -> 0% of each run, Pallas kernels for 0% -> 0%
where the time goes in v1:
time: 129 us
  Pallas kernels  115 us (89%)
  local copies, waits for them, and re-layouts  11.6 us (9%)
  other arithmetic  1.29 us (1%)
    pallas_call x1, Pallas kernels, on_device(): pl.pallas_call(functools.partial(kernel, scale), out_shape=(shape((TB, FB...  115 us
    unnamed x19, local copies, waits for them, and re-layouts  10.3 us

profile of v1, /device:TPU:2, one launch (start us, length us, event | category | flops | bytes accessed | tf_op | source)
XLA Modules:
  0.0 128.9 jit_solution(10558271045710016944)
XLA Ops:
  0.6 0.0 copy-start.2
  0.6 1.3 %broadcast_in_dim.10.ubias = f32[1,768]{1,0:T(1,128)} reshape(f32[768]{0:T(1024)} %param.10) | data formatting | bytes 6144 | tf_op jit(solution)/shard_map/broadcast_in_dim | solution.py:688
  2.0 1.7 %copy.14.patches = bf16[256,192]{1,0:T(8,128)(2,1)} copy(bf16[256,192]{0,1:T(8,128)(2,1)} %param.7) | data formatting | bytes 196608 | tf_op args[0]
  3.6 1.7 %copy.16.cot = bf16[256,192]{1,0:T(8,128)(2,1)} copy(bf16[256,192]{0,1:T(8,128)(2,1)} %param.13) | data formatting | bytes 196608 | tf_op args[6]
  5.3 0.0 copy-done.2
  5.3 0.9 copy.15.w2in
  6.2 115.3 %mlp_block.1 = (bf16[256,192]{1,0:T(8,128)(2,1)}, bf16[256,192]{1,0:T(8,128)(2,1)}, f32[1,192]{1,0:T(1,128)}, bf16[192,768]{1,0:T(8,128)(2,1)}, f32[1,768]{1,0:T...) custom-call(bf16[256,192]{1,0:T(8,128)(2,1)} %copy.14.patches, f32[1,192]{1,0:T(1,128)} %bitcast.4, ...), custom_call_target="tpu_custom_call" | custom-call | tf_op jit(solution)/shard_map/mlp_block/pallas_call | solution.py:675
  121.5 0.0 copy-start
  121.5 1.7 %copy.17 = bf16[256,192]{0,1:T(8,128)(2,1)} copy(bf16[256,192]{1,0:T(8,128)(2,1)} %get-tuple-element.21) | data formatting | bytes 196608
  123.2 1.3 reduce
  124.5 1.6 %copy.18 = bf16[256,192]{0,1:T(8,128)(2,1)} copy(bf16[256,192]{1,0:T(8,128)(2,1)} %get-tuple-element.22) | data formatting | bytes 196608
  126.1 0.0 copy-done
  126.1 0.0 copy-start.4
  126.1 0.0 copy-start.1
  126.1 0.9 copy.19
  127.0 0.0 copy-done.4
  127.0 0.6 copy.23
  127.6 0.0 copy-done.1
  127.6 0.0 copy-start.3
  127.6 0.7 copy.24
  128.3 0.0 copy-done.3
  128.3 0.6 copy.25
Async XLA Ops:
  0.6 4.6 %copy-start.2 = (bf16[768,192]{0,1:T(8,128)(2,1)S(1)}, bf16[768,192]{0,1:T(8,128)(2,1)}, u32[]{:S(2)}) copy-start(bf16[768,192]{0,1:T(8,128)(2,1)} %param.11) | copy-start | bytes 884740
  121.5 4.6 %copy-start = (bf16[768,192]{1,0:T(8,128)(2,1)S(1)}, bf16[768,192]{1,0:T(8,128)(2,1)}, u32[]{:S(2)}) copy-start(bf16[768,192]{1,0:T(8,128)(2,1)} %get-tuple-element.26) | copy-start | bytes 884740
  126.1 0.9 copy-start.4
  126.1 1.4 %copy-start.1 = (bf16[192,768]{1,0:T(8,128)(2,1)S(1)}, bf16[192,768]{1,0:T(8,128)(2,1)}, u32[]{:S(2)}) copy-start(bf16[192,768]{1,0:T(8,128)(2,1)} %get-tuple-element.38) | copy-start | bytes 884740
  127.6 0.7 copy-start.3

commit v2 on v0

v2 whole, which is shorter than its diff:
```python
import functools
import math

import jax
import jax.numpy as jnp
from jax import lax
from jax.experimental import pallas as pl
from jax.experimental.pallas import tpu as pltpu
from jax.sharding import PartitionSpec as P

MESH = pl.DeviceIdType.MESH
BF = jnp.bfloat16
F32 = jnp.float32

NB = 16
FB = 192
TB = 256
HB = 384
D = NB * FB
N_SEM = 320
ORDER = (
    0, 34, 1, 45, 17, 18, 35, 46, 9, 3, 2, 39, 36, 11, 10, 20, 4, 47, 13, 5, 26, 38, 12, 56, 37, 19, 15, 44,
    14, 7, 6, 50, 49, 27, 48, 28, 40, 22, 21, 16, 43, 57, 55, 41, 52, 42, 51, 8, 59, 30, 29, 58, 60, 62, 23,
    54, 24, 53, 63, 32, 31, 61, 64, 66, 25, 33, 149, 65, 116, 115, 86, 83, 67, 150, 88, 87, 119, 151, 68, 85,
    152, 110, 136, 133, 153, 132, 107, 104, 122, 112, 111, 134, 91, 121, 109, 94, 139, 69, 138, 97, 120, 93,
    108, 117, 100, 137, 92, 106, 70, 123, 101, 84, 80, 96, 125, 154, 105, 124, 95, 128, 141, 103, 82, 142,
    140, 99, 155, 156, 72, 73, 102, 145, 127, 98, 118, 113, 81, 77, 126, 76, 130, 143, 71, 79, 75, 135, 147,
    144, 114, 78, 157, 74, 89, 129, 159, 158, 146, 131, 160, 148, 90,
)


def tag(*parts):
    return "".join(map(str, parts))


def rem(a, n):
    return lax.rem(a, n)


def nn_dot(left, right):
    return jnp.dot(left, right, preferred_element_type=F32)


def kernel(
    scale,
    patches, gain, w1in, ubias, w2in, dbias, cot,
    mixed_o, pgrad_o, gaing_o, dw1_o, ubg_o, dw2_o, dbg_o,
    XT, XN, CT, W1, W2, W1H, W2H,
    GIN, UIN, DIN, GA, UB, BC, GW, MI,
    PRE, SL, HG, HID, PG, HIDR, PGR,
    MX, MXS, MXP, MXM, MXT,
    NG, NGS, NGP, NGM, NGT,
    G1, G1Y, G1X, G1T, G1F,
    G2, G2Y, G2X, G2T, G2F,
    ST, STS, STZ, STT,
    MS, RM, UT, FU, GT, GTX, GTY,
    MO, PO, GO, UO, DO,
    ss, rs, ls,
):
    r = lax.axis_index("row")
    c = lax.axis_index("col")
    x, y = r // 4, rem(r, 4)
    z, k = c // 2, rem(c, 2)
    g = y // 2
    yh = y + 1 - 2 * rem(y, 2)
    yt = 3 - y
    yq = 3 - yh
    own = g == k
    other = g != k

    def dev(xx, yy, zz, kk):
        return (xx * 4 + yy, zz * 2 + kk)

    def zdev(j):
        return dev(x, y, rem(z + j + 8, 8), k)

    def xdev(j):
        return dev(rem(x + j + 4, 4), y, z, k)

    sib = dev(x, y, z, 1 - k)
    hdev = dev(x, yh, z, k)
    tdev = dev(x, yt, z, k)
    tdev2 = dev(x, yt, z, 1 - k)
    zp, zm, xp, xm = zdev(1), zdev(-1), xdev(1), xdev(-1)

    def zb(j, kk):
        return rem(z + j + 8, 8) * 2 + kk

    def wb(j, yy):
        return rem(x + j + 4, 4) * 4 + yy

    b0 = zb(0, k)

    barrier = pltpu.get_barrier_semaphore()
    peers = [zdev(j) for j in range(1, 8)] + [xdev(j) for j in range(1, 4)]
    peers += [dev(x, rem(y + j, 4), z, k) for j in range(1, 4)]
    peers += [dev(rem(x + j, 4), yh, z, k) for j in range(1, 4)]
    peers += [sib, tdev2]
    for peer in peers:
        pl.semaphore_signal(barrier, inc=1, device_id=peer, device_id_type=MESH)

    ids = {}
    made = {}
    seen = set()

    def sem(name):
        return ids.setdefault(name, len(ids))

    def rc(sname, rname, src, dst, to):
        return pltpu.make_async_remote_copy(
            src_ref=src, dst_ref=dst, send_sem=ss.at[sem(sname)], recv_sem=rs.at[sem(rname)],
            device_id=to, device_id_type=MESH,
        )

    def send(name, src, dst, to):
        copy = rc(name, name, src, dst, to)
        copy.start()
        made[name] = copy

    def got(*names):
        for name in names:
            if name not in seen:
                seen.add(name)
                made[name].wait_recv()

    local = {}

    def copy_in(name, src, dst):
        local[name] = pltpu.make_async_copy(src, dst, ls.at[len(local)])
        local[name].start()

    copy_in("X", patches, XT.at[0, b0])
    copy_in("V0", w1in.at[:, 0:HB], W1H.at[0])
    copy_in("V1", w1in.at[:, HB:2 * HB], W1H.at[1])
    copy_in("U0", w2in.at[:, 0:HB], W2H.at[0])
    copy_in("U1", w2in.at[:, HB:2 * HB], W2H.at[1])
    copy_in("C", cot, CT.at[0, b0])
    copy_in("g", gain, GIN)
    copy_in("u", ubias, UIN)
    copy_in("d", dbias, DIN)

    tasks = {}

    def task(name, run, *after):
        assert name not in tasks
        tasks[name] = (run, after)

    def gather_tokens(t, A):
        def edge():
            local[t].wait()
            send(t + "T", A.at[0, b0], A.at[1, b0], tdev)

        def first(s):
            if s:
                got(t + "T")
            send(tag(t, "p1", s), A.at[s, b0], A.at[s, b0], zp)
            send(tag(t, "m1", s), A.at[s, b0], A.at[s, b0], zm)
            send(tag(t, "sib0", s), A.at[s, b0], A.at[s, b0], sib)

        def relay(s, n, way):
            b, to, part = (zb(-n, k), zp, lo) if way == "p" else (zb(n, k), zm, hi)
            got(tag(t, way, n, s))
            src = A.at[s, b] if n < 3 else A.at[s, b, part]
            send(tag(t, way, n + 1, s), src, src, to)
            send(tag(t, "sib", way, n, s), A.at[s, b], A.at[s, b], sib)

        def last(s):
            b4 = zb(4, k)
            got(tag(t, "p4", s), tag(t, "m4", s))
            send(tag(t, "sib4", s), A.at[s, b4], A.at[s, b4], sib)

        task(t + "T", edge)
        for s in range(2):
            task(tag(t, "f", s), functools.partial(first, s), t + "T")
            for n in range(1, 4):
                for way in "pm":
                    task(tag(t, way, n, s), functools.partial(relay, s, n, way))
            task(tag(t, "l", s), functools.partial(last, s))

    def tokens_here(t, s):
        for n in ("0", "p1", "m1", "p2", "m2", "p3", "m3", "4"):
            got(tag(t, "sib", n, s))

    lo, hi = pl.ds(0, FB // 2), pl.ds(FB // 2, FB // 2)
    r0, rt, rq = wb(0, y), wb(0, yt), wb(0, yq)

    def gather_panel(t, WH, W):
        def start():
            local[t + "0"].wait()
            local[t + "1"].wait()

            @pl.when(own)
            def _():
                W[r] = WH[k]
                rc(t + "b", t + "u0", WH.at[1 - k], W.at[r], sib).start()

            @pl.when(other)
            def _():
                rc(t + "a", t + "u1", WH.at[k], W.at[r], tdev).start()
                rc(t + "b", t + "u1", WH.at[1 - k], W.at[r], tdev2).start()


        def spread0():
            @pl.when(other)
            def _():
                rc(t + "b", t + "u0", WH.at[1 - k], W.at[r], sib).wait_recv()

            send(t + "P+", W.at[r0], W.at[r0], xp)
            send(t + "P-", W.at[r0], W.at[r0], xm)
            send(t + "Y0", W.at[r0], W.at[r0], hdev)

        def spread1():
            rc(t + "a", t + "u1", WH.at[k], W.at[rt], tdev).wait_recv()
            send(t + "Q0", W.at[rt], W.at[rt], hdev)
            send(t + "Q+", W.at[rt], W.at[rt], xp)
            send(t + "Q-", W.at[rt], W.at[rt], xm)

        def spread2():
            got(t + "Q0")
            send(t + "R+", W.at[rq], W.at[rq], xp)
            send(t + "R-", W.at[rq], W.at[rq], xm)

        def relay(n, yy, way):
            b, to, part, y_name = (wb(-1, yy), xp, lo, "Y1") if way == "+" else (wb(1, yy), xm, hi, "Y2")
            got(tag(t, n, way))
            send(tag(t, n, "2", way), W.at[b, part], W.at[b, part], to)
            if n == "P":
                send(t + y_name, W.at[b], W.at[b], hdev)

        def last():
            b = wb(2, y)
            got(t + "P2+", t + "P2-")
            send(t + "Y3", W.at[b], W.at[b], hdev)

        task(t + "s", start)
        task(t + "0", spread0, t + "s")
        task(t + "1", spread1, t + "s")
        task(t + "2", spread2, t + "s")
        for n, yy in (("P", y), ("Q", yt), ("R", yq)):
            for way in "+-":
                task(t + n + way, functools.partial(relay, n, yy, way))
        task(t + "l", last)

    def panel_here(t):
        got(*(t + n for n in ("Q2+", "Q2-", "R2+", "R2-", "Y0", "Y1", "Y2", "Y3")))

    gather_tokens("X", XT)
    gather_tokens("C", CT)
    gather_panel("V", W1H, W1)
    gather_panel("U", W2H, W2)

    def small_start():
        for name in "gud":
            local[name].wait()
        GA[k, z] = jnp.zeros((1, 256), F32)
        GA[k, z, :, 0:FB] = GIN[...]
        halves = [jnp.concatenate([UIN[i:i + 1] for i in range(n, n + 3)], axis=1) for n in (0, 3)]
        UB[k] = halves[0]
        UB[1 - k] = halves[1]
        send("ub", UB.at[1], UB.at[2], sib)
        for j in range(1, 8):
            send(tag("ga", j), GA.at[k, z], GA.at[k, z], zdev(j))

    def small_next():
        for j in range(1, 8):
            got(tag("ga", j))
        send("gas", GA.at[k], GA.at[k], sib)

    task("ga", small_start)
    task("gb", small_next, "ga")

    def blocks_sum(slot, term):
        def step(b, total):
            return total + term(XT[slot, b].astype(F32)).reshape(FB // 8, 8, TB).sum(0)

        total = lax.fori_loop(0, NB, step, jnp.zeros((8, TB), F32))
        return jnp.sum(total, axis=0, keepdims=True)

    def statistics(slot):
        tokens_here("X", slot)
        mean = blocks_sum(slot, lambda v: v) / D
        var = blocks_sum(slot, lambda v: (v - mean) * (v - mean)) / D
        MI[slot, 0:1] = mean
        MI[slot, 1:2] = lax.rsqrt(var + 1e-06)

    def gain_column(kk, zz):
        return jnp.broadcast_to(GA[kk, zz], (8, 256)).T[:FB, 0:1]

    def normalise(part):
        got("gas", "ub")

        def block(b, carry):
            column = gain_column(rem(b, 2), b // 2)
            for slot in range(2):
                v = (XT[slot, b].astype(F32) - MI[slot, 0:1]) * MI[slot, 1:2]
                XN[slot, b] = (v * column).astype(BF)
            return carry

        lax.fori_loop(part * 4, part * 4 + 4, block, 0)

    task("st0", functools.partial(statistics, 0), "Xl0")
    task("st1", functools.partial(statistics, 1), "Xl1")
    for part in range(4):
        task(tag("nm", part), functools.partial(normalise, part), "st0", "st1", "gb")

    GRP = 4

    def panel_dot(W, A, out):
        for j in range(NB // GRP):
            wt = W[j * GRP:(j + 1) * GRP].reshape(GRP * FB, HB).T
            for slot in range(2):
                part = nn_dot(wt, A[slot, j * GRP:(j + 1) * GRP].reshape(GRP * FB, TB))
                if j == 0:
                    out[slot] = part
                else:
                    out[slot] += part

    def first_product():
        panel_here("V")
        panel_dot(W1, XN, PRE)
        bias = jnp.where(own, UB[0], UB[2])
        BC[...] = jnp.broadcast_to(jnp.broadcast_to(bias, (8, HB)).T[:, 0:1], (HB, 128))

    CH = 64

    def gelu_rows(slot, i, carry):
        rows = pl.ds(pl.multiple_of(i * CH, CH), CH)
        v = PRE[slot, rows] + jnp.concatenate([BC[rows]] * 2, axis=1)
        cdf = 0.5 * (1.0 + lax.erf(v * 0.7071067811865476))
        HID[slot, rows] = (v * cdf).astype(BF)
        SL[slot, rows] = cdf + v * jnp.exp(-0.5 * v * v) * 0.3989422804014327
        return carry

    def gelu(slot):
        lax.fori_loop(0, HB // CH, functools.partial(gelu_rows, slot), 0)
        HIDR[slot] = HID[slot].T

    task("pre", first_product, "nm0", "nm1", "nm2", "nm3", "V0", "V1", "V2", "Vl", "VP+", "VP-", "VQ+", "VQ-", "VR+", "VR-")
    task("ge0", functools.partial(gelu, 0), "pre")
    task("ge1", functools.partial(gelu, 1), "pre")

    def scatter_tokens(t, W, A, M, S, RP, RN, RT, finish, *after):
        def make(j):
            if t == "M":
                panel_here("U")
            pair = rem(z + j + 8, 8)
            w = W[pl.ds(pl.multiple_of(pair * 2, 2), 2)].reshape(2 * FB, HB)
            for slot in range(2):
                part = nn_dot(w, A[slot]).astype(BF)
                M[slot, pair * 2] = part[:FB]
                M[slot, pair * 2 + 1] = part[FB:]
            send(tag(t, "s", j), M.at[:, pair * 2 + 1 - k], S.at[j + 3], sib)

        def relay(j, slot):
            b = zb(j, k)
            got(tag(t, "s", j))
            total = M[slot, b].astype(F32) + S[j + 3, slot].astype(F32)
            if j == 3 and slot == 0 or j in (1, 2):
                got(tag(t, "+", j + 1, slot))
                total = total + RP[slot, 3 - j].astype(F32)
            if j == -3 and slot == 1 or j in (-1, -2):
                got(tag(t, "-", 1 - j, slot))
                total = total + RN[slot, 3 + j].astype(F32)
            M[slot, b] = total.astype(BF)
            if j > 0 and (j < 4 or slot == 0):
                send(tag(t, "+", j, slot), M.at[slot, b], RP.at[slot, 4 - j], zp)
            else:
                n = abs(j)
                send(tag(t, "-", n, slot), M.at[slot, b], RN.at[slot, 4 - n], zm)

        def summed(slot):
            got(tag(t, "s0"), tag(t, "+1", slot), tag(t, "-1", slot))
            total = M[slot, b0].astype(F32) + S[3, slot].astype(F32)
            return total + RP[slot, 3].astype(F32) + RN[slot, 3].astype(F32)

        def edge():
            M[1, b0] = summed(1).astype(BF)
            send(t + "T", M.at[1, b0], RT, tdev)

        def final():
            total = summed(0)
            got(t + "T")
            finish(total + RT[...].astype(F32))

        for j in range(-3, 5):
            task(tag(t, "k", j), functools.partial(make, j), *after)
            for slot in range(2):
                if j:
                    task(tag(t, j, ".", slot), functools.partial(relay, j, slot), tag(t, "k", j))
        task(t + "e", edge, t + "k0")
        task(t + "f", final, t + "k0")

    def finish_mixed(total):
        shift = jnp.broadcast_to(DIN[...], (8, FB)).T[:, 0:1]
        MO[...] = (XT[0, b0].astype(F32) + total + shift).astype(BF)
        copy_in("mo", MO, mixed_o)

    def finish_grad(grad):
        got("stt")
        sums = ST[2, 0] + STT[...]
        inv_std = MI[0, 1:2]
        normed = (XT[0, b0].astype(F32) - MI[0, 0:1]) * inv_std
        product = jnp.sum((grad * normed).T, axis=0, keepdims=True)
        GT[0] = jnp.zeros((1, 256), F32)
        GT[0, :, 0:FB] = product
        for j in range(1, 4):
            send(tag("gx", j), GT.at[0], GTX.at[j], xdev(j))
        correction = grad * gain_column(k, z) - sums[0:1] / D - normed * (sums[1:2] / D)
        PO[...] = (CT[0, b0].astype(F32) + inv_std * correction).astype(BF)
        copy_in("po", PO, pgrad_o)

    UDONE = ("U0", "U1", "U2", "Ul", "UP+", "UP-", "UQ+", "UQ-", "UR+", "UR-")
    scatter_tokens("M", W2, HID, MX, MXS, MXP, MXM, MXT, finish_mixed, "ge0", "ge1", *UDONE)
    scatter_tokens("N", W1, PG, NG, NGS, NGP, NGM, NGT, finish_grad, "sl0", "sl1")

    def deliver(t, T0, T1, out):
        @pl.when(own)
        def _():
            out[k] = T0[...]
            rc(t + "f1", t + "q1", T1, out.at[k], tdev).start()

        @pl.when(other)
        def _():
            rc(t + "f0", t + "q0", T0, out.at[k], sib).start()
            rc(t + "f1", t + "q2", T1, out.at[k], tdev2).start()

    def delivered(t, T0, T1, out):
        @pl.when(own)
        def _():
            rc(t + "f0", t + "q0", T0, out.at[1 - k], sib).wait_recv()

        @pl.when(other)
        def _():
            rc(t + "f1", t + "q1", T1, out.at[k], tdev).wait_recv()
            rc(t + "f1", t + "q2", T1, out.at[1 - k], tdev2).wait_recv()

    def departed(t, T0, T1, out):
        rc(t + "f1", t + "q1", T1, out.at[k], tdev).wait_send()

        @pl.when(other)
        def _():
            rc(t + "f0", t + "q0", T0, out.at[k], sib).wait_send()

    def scatter_panel(t, A, B, G, RY, RX, T, F, out, *after):
        made_here = set()

        def make(*blocks):
            if t == "D":
                tokens_here("C", 0)
                tokens_here("C", 1)
            for j, yy in blocks:
                b = wb(j, yy)
                part = nn_dot(A[0, b], B[0]) + nn_dot(A[1, b], B[1])
                G[b] = (part * scale).astype(BF)

        def hid(j):
            make((j, yh))
            send(tag(t, "h", j), G.at[wb(j, yh)], RY.at[j + 1], hdev)

        def far(n, i, yy):
            make((2, yy))
            b = wb(2, yy)
            if n == "o":
                add(2)
            send(tag(t, n, "2+"), G.at[b, lo], RX.at[i, 0, lo], xp)
            send(tag(t, n, "2-"), G.at[b, hi], RX.at[i, 0, hi], xm)

        def add(j):
            b = wb(j, y)
            got(tag(t, "h", j))
            G[b] = (G[b].astype(F32) + RY[j + 1].astype(F32)).astype(BF)

        def near(n, i, yy, j):
            to, way, part = (xp, "+", lo) if j > 0 else (xm, "-", hi)
            b = wb(j, yy)
            make((j, yy))
            if n == "o":
                add(j)
            got(tag(t, n, "2", way))
            G[b, part] = (G[b, part].astype(F32) + RX[i, 0, part].astype(F32)).astype(BF)
            send(tag(t, n, "1", way), G.at[b], RX.at[i, 1 if j > 0 else 2], to)

        def total(n, i, yy):
            make((0, yy))
            got(tag(t, n, "1+"), tag(t, n, "1-"))
            return G[wb(0, yy)].astype(F32) + RX[i, 1].astype(F32) + RX[i, 2].astype(F32)

        def total_w():
            T[0] = total("w", 1, yq).astype(BF)
            send(t + "w", T.at[0], RY.at[4], hdev)

        def total_o():
            got(tag(t, "h0"))
            T[1] = (total("o", 0, y) + RY[1].astype(F32)).astype(BF)

            @pl.when(own)
            def _():
                F[k] = T[1]

            @pl.when(other)
            def _():
                rc(t + "f0", t + "q0", T.at[1], F.at[k], sib).start()


        def total_t():
            part = total("t", 2, yt)
            got(t + "w")
            T[2] = (part + RY[4].astype(F32)).astype(BF)

            @pl.when(own)
            def _():
                rc(t + "f1", t + "q1", T.at[2], F.at[k], tdev).start()

            @pl.when(other)
            def _():
                rc(t + "f1", t + "q2", T.at[2], F.at[k], tdev2).start()


        def final():
            delivered(t, T.at[1], T.at[2], F)
            copy_in(t + "o0", F.at[0], out.at[:, 0:HB])
            copy_in(t + "o1", F.at[1], out.at[:, HB:2 * HB])

        for j in (2, 1, -1, 0):
            task(tag(t, "h", j), functools.partial(hid, j), *after)
        for n, i, yy in (("w", 1, yq), ("t", 2, yt), ("o", 0, y)):
            task(tag(t, n, "2"), functools.partial(far, n, i, yy), *after)
            for j in (1, -1):
                task(tag(t, n, j), functools.partial(near, n, i, yy, j), *after)
        task(t + "tw", total_w, *after)
        task(t + "to", total_o, *after)
        task(t + "tt", total_t, *after)
        task(t + "f", final, t + "to", t + "tt")

    scatter_panel("D", CT, HIDR, G2, G2Y, G2X, G2T, G2F, dw2_o, "ge0", "ge1", "Cl0", "Cl1")
    scatter_panel("E", XN, PGR, G1, G1Y, G1X, G1T, G1F, dw1_o, "sl0", "sl1")

    def gain_weight():
        def step(b, total):
            column = gain_column(rem(b, 2), b // 2)
            return total + (W1[b].astype(F32) * column).reshape(FB // 8, 8, HB).sum(0)

        got("gas")
        panel_here("V")
        gw = lax.fori_loop(0, NB, step, jnp.zeros((8, HB), F32))
        gw = jnp.broadcast_to(jnp.sum(gw, axis=0, keepdims=True), (8, HB))
        GW[...] = jnp.broadcast_to(gw.T[:, 0:1], (HB, 128))

    def second_product():
        tokens_here("C", 0)
        tokens_here("C", 1)
        panel_here("U")
        panel_dot(W2, CT, HG)

    def slope_rows(slot, i, sums):
        first, second = sums
        rows = pl.ds(pl.multiple_of(i * CH, CH), CH)
        grad = (HG[slot, rows] * SL[slot, rows]).astype(BF)
        PG[slot, rows] = grad
        wide = grad.astype(F32)
        first += (wide * jnp.concatenate([GW[rows]] * 2, axis=1)).reshape(CH // 8, 8, TB).sum(0)
        second += (wide * PRE[slot, rows]).reshape(CH // 8, 8, TB).sum(0)
        return first, second

    up_sums = []

    def slope(slot):
        zero = jnp.zeros((8, TB), F32)
        first, second = lax.fori_loop(0, HB // CH, functools.partial(slope_rows, slot), (zero, zero))
        ST[0, slot, 0:1] = jnp.sum(first, axis=0, keepdims=True)
        ST[0, slot, 1:2] = jnp.sum(second, axis=0, keepdims=True)
        turned = PG[slot].T
        PGR[slot] = turned
        up_sums.append(jnp.sum(turned.astype(F32), axis=0, keepdims=True))

    task("gw", gain_weight, "gb", "pre")
    task("hg", second_product, "Cl0", "Cl1", *UDONE)
    task("sl0", functools.partial(slope, 0), "hg", "ge0", "gw")
    task("sl1", functools.partial(slope, 1), "hg", "ge1", "gw")

    def sums_pair():
        send("st", ST.at[0], STS, sib)

    def sums_z():
        got("st")
        ST[1] = ST[0] + STS[...]
        for j in range(1, 8):
            send(tag("st", j), ST.at[1], STZ.at[j], zdev(j))

    def sums_edge():
        total = ST[1]
        for j in range(1, 8):
            got(tag("st", j))
            total = total + STZ[j]
        ST[2] = total
        send("stt", ST.at[2, 1], STT, tdev)

    task("sa", sums_pair, "sl0", "sl1")
    task("sb", sums_z, "sa")
    task("sc", sums_edge, "sb")

    peers8 = [(j, h) for j in range(4) for h in range(2)]

    def bias_row(b):
        v = CT[0, b].astype(F32) + CT[1, b].astype(F32)
        return jnp.sum((v[:, :128] + v[:, 128:]).T, axis=0, keepdims=True)

    def bias_send():
        for i, (j, h) in enumerate(peers8):
            yy = yh if h else y
            MS[i, :, 0:HB] = up_sums[0] + up_sums[1]
            MS[i, :, HB:HB + 256] = jnp.zeros((1, 256), F32)
            MS[i, :, HB:HB + FB] = bias_row(wb(j, yy))
            if i:
                send(tag("ms", i), MS.at[i], RM.at[i], dev(rem(x + j, 4), yy, z, k))

    def bias_sum():
        total = MS[0]
        for i in range(1, 8):
            got(tag("ms", i))
            total = total + RM[i]
        UT[...] = total[:, :HB]
        DO[...] = total[0:1, HB:HB + FB] * scale
        deliver("B", UT, UT, FU)
        copy_in("do", DO, dbg_o)

    def bias_final():
        delivered("B", UT, UT, FU)
        for i in range(6):
            UO[i:i + 1] = FU[i // 3, 0:1, i % 3 * 128:i % 3 * 128 + 128] * scale
        copy_in("uo", UO, ubg_o)

    task("ba", bias_send, "sl0", "sl1", "hg")
    task("bb", bias_sum, "ba")
    task("bc", bias_final, "bb")

    def gain_y():
        total = GT[0]
        for j in range(1, 4):
            got(tag("gx", j))
            total = total + GTX[j]
        GT[1] = total
        for j in range(1, 4):
            send(tag("gy", j), GT.at[1], GTY.at[j], dev(x, rem(y + j, 4), z, k))

    def gain_final():
        total = GT[1]
        for j in range(1, 4):
            got(tag("gy", j))
            total = total + GTY[j]
        GO[...] = total[0:1, :FB] * scale
        copy_in("go", GO, gaing_o)

    task("gy", gain_y, "Nf")
    task("gz", gain_final, "gy")

    pl.semaphore_wait(barrier, len(peers))
    done = set()
    names = list(tasks)
    for name in (names[i] for i in ORDER):
        run, after = tasks[name]
        assert done.issuperset(after), name
        run()
        done.add(name)
    assert len(done) == len(tasks)

    for name in ("mo", "po", "go", "uo", "do", "Do0", "Do1", "Eo0", "Eo1"):
        local[name].wait()
    for copy in made.values():
        copy.wait_send()
    for t, WH, W in (("V", W1H, W1), ("U", W2H, W2)):
        rc(t + "b", t + "u0", WH.at[1 - k], W.at[r], sib).wait_send()

        @pl.when(other)
        def _(t=t, WH=WH, W=W):
            rc(t + "a", t + "u1", WH.at[k], W.at[r], tdev).wait_send()

    departed("D", G2T.at[1], G2T.at[2], G2F)
    departed("E", G1T.at[1], G1T.at[2], G1F)
    departed("B", UT, UT, FU)
    assert len(ids) <= N_SEM


def hand_over(*refs):
    n = len(refs) // 2
    copies = [pltpu.make_async_copy(refs[i], refs[n + i], refs[-1].at[i]) for i in range(n)]
    for copy in copies:
        copy.start()
    for copy in copies:
        copy.wait()


def on_device(patches, norm_gain, up_weight, up_bias, down_weight, down_bias, cotangent):
    scale = 1.0 / math.sqrt(patches.shape[0] * lax.axis_size("row"))
    vm = pltpu.VMEM
    tokens = vm((2, NB, FB, TB), BF)
    panel = vm((NB, FB, HB), BF)
    tile = vm((2, HB, TB), F32)
    ring = vm((2, 4, FB, TB), BF)
    scatter_z = [tokens, vm((8, 2, FB, TB), BF), ring, ring, vm((FB, TB), BF)]
    scatter_w = [panel, vm((5, FB, HB), BF), vm((3, 3, FB, HB), BF), vm((3, FB, HB), BF), vm((2, FB, HB), BF)]
    scratch = [
        tokens, tokens, tokens, panel, panel, vm((2, FB, HB), BF), vm((2, FB, HB), BF),
        vm((1, FB), F32), vm((6, 128), F32), vm((1, FB), F32),
        vm((2, 8, 1, 256), F32), vm((3, 1, HB), F32), vm((HB, 128), F32), vm((HB, 128), F32), vm((2, 8, TB), F32),
        tile, tile, tile, vm((2, HB, TB), BF), vm((2, HB, TB), BF), vm((2, TB, HB), BF), vm((2, TB, HB), BF),
        *scatter_z, *scatter_z, *scatter_w, *scatter_w,
        vm((3, 2, 2, TB), F32), vm((2, 2, TB), F32), vm((8, 2, 2, TB), F32), vm((2, TB), F32),
        vm((8, 1, HB + 256), F32), vm((8, 1, HB + 256), F32), vm((1, HB), F32), vm((2, 1, HB), F32),
        vm((2, 1, 256), F32), vm((4, 1, 256), F32), vm((4, 1, 256), F32),
        vm((FB, TB), BF), vm((FB, TB), BF), vm((1, FB), F32), vm((6, 128), F32), vm((1, FB), F32),
        pltpu.SemaphoreType.DMA((N_SEM,)), pltpu.SemaphoreType.DMA((N_SEM,)), pltpu.SemaphoreType.DMA((24,)),
    ]
    shape = jax.ShapeDtypeStruct
    whole = pl.BlockSpec(memory_space=pl.ANY)
    results = (
        shape((FB, TB), BF), shape((FB, TB), BF), shape((1, FB), F32), shape((FB, 2 * HB), BF),
        shape((2 * HB // 128, 128), F32), shape((FB, 2 * HB), BF), shape((1, FB), F32),
    )
    parts = pl.pallas_call(
        functools.partial(kernel, scale),
        out_shape=results,
        in_specs=[whole] * 7,
        out_specs=(whole,) * 7,
        scratch_shapes=scratch,
        compiler_params=pltpu.CompilerParams(
            collective_id=0, has_side_effects=True, vmem_limit_bytes=60 << 20
        ),
        name="mlp_block",
    )(
        patches.T, norm_gain[None, :], up_weight, up_bias.reshape(2 * HB // 128, 128),
        down_weight.T, down_bias[None, :], cotangent.T,
    )
    mixed, patch_grad, gain_grad, up_grad, up_bias_grad, down_grad, down_bias_grad = pl.pallas_call(
        hand_over,
        out_shape=results,
        in_specs=[pl.BlockSpec(memory_space=pltpu.VMEM)] * 7,
        out_specs=(whole,) * 7,
        scratch_shapes=[pltpu.SemaphoreType.DMA((7,))],
        name="hand_over",
    )(*parts)
    return (
        mixed.T, patch_grad.T, gain_grad[0], up_grad, up_bias_grad.reshape(2 * HB), down_grad.T, down_bias_grad[0],
    )


def solution(mesh):
    in_specs = (
        P("row", "col"),
        P("col"),
        P("row", "col"),
        P("col"),
        P("col", "row"),
        P("col"),
        P("row", "col"),
    )
    out_specs = (
        P("row", "col"),
        P("row", "col"),
        P("col"),
        P("row", "col"),
        P("col"),
        P("col", "row"),
        P("row"),
    )
    return jax.shard_map(
        on_device, mesh=mesh, in_specs=in_specs, out_specs=out_specs, check_vma=False
    )
```

time: 603 us -> 97.1 us (0.16)
  waiting for transfers between devices: 438 us -> 0 us
  blocking collectives: 112 us -> 0 us
  Pallas kernels: 0 us -> 96.2 us
  matrix products: 27.2 us -> 0 us
  between operations: 13.9 us -> 0.8 us
  other arithmetic: 9.03 us -> 0 us
    reduce_scatter x4 -> x0, waiting for transfers between devices: 230 us -> none  [the longest x1 87.1 us: on_device(): lax.psum_scatter(down_term.astype(jnp.bfloat16), 'row', scatter_dimension...]
    all_gather x4 -> x0, waiting for transfers between devices: 149 us -> none  [the longest x1 60.2 us: on_device(): up_panel = lax.all_gather(up_weight, 'row', axis=0, tiled=True)]
    psum x4 -> x0, blocking collectives: 112 us -> none  [the longest x1 35.4 us: on_device(): lax.psum((grad_scale * jnp.sum(pre_grad, axis=0, dtype=jnp.float32), grad...]
    pallas_call x0 -> x2, Pallas kernels: none -> 96.2 us  [the longest x1 94.1 us: on_device(): pl.pallas_call(functools.partial(kernel, scale), out_shape=results, in_sp...]
    unnamed x10 -> x0, waiting for transfers between devices: 59.2 us -> none
    dot_general x6 -> x0, matrix products: 27.2 us -> none  [the longest x2 9.99 us: contract_first(): lax.dot_general(left, right, (((0,), (0,)), ((), ())), preferred_element_...]
  transfers between devices with their start and end apart: 9 -> 0, of which waited for: 7 -> 0; matrix products, arithmetic and copies ran while one was open for 6% -> 0% of each run, Pallas kernels for 0% -> 0%
where the time goes in v2:
time: 97.1 us; the launch traced here: 97 us
  Pallas kernels  96.2 us (99%)
    pallas_call x1, Pallas kernels, on_device(): pl.pallas_call(functools.partial(kernel, scale), out_shape=results, in_sp...  94.1 us
    pallas_call x1, Pallas kernels, on_device(): pl.pallas_call(hand_over, out_shape=results, in_specs=[pl.BlockSpec(memor...  2.08 us

profile of v2, /device:TPU:2, one launch (start us, length us, event | category | flops | bytes accessed | tf_op | source)
XLA Modules:
  0.0 97.0 jit_solution(9040128866616068151)
XLA Ops:
  0.6 94.1 %mlp_block.1 = (bf16[192,256]{1,0:T(8,128)(2,1)}, bf16[192,256]{1,0:T(8,128)(2,1)}, f32[1,192]{1,0:T(1,128)}, bf16[192,768]{1,0:T(8,128)(2,1)}, f32[6,128]{1,0:T...) custom-call(bf16[192,256]{1,0:T(8,128)(2,1)} %bitcast.13, f32[1,192]{1,0:T(1,128)} %bitcast.16, ...), custom_call_target="tpu_custom_call" | custom-call | tf_op jit(solution)/shard_map/mlp_block/pallas_call | solution.py:720
  94.7 2.1 %hand_over.1 = (bf16[192,256]{1,0:T(8,128)(2,1)}, bf16[192,256]{1,0:T(8,128)(2,1)}, f32[1,192]{1,0:T(1,128)}, bf16[192,768]{1,0:T(8,128)(2,1)}, f32[6,128]{1,0:T...) custom-call(bf16[192,256]{1,0:T(8,128)(2,1)} %get-tuple-element.21.refs_0_, ...), custom_call_target="tpu_custom_call" | custom-call | tf_op jit(solution)/shard_map/hand_over/pallas_call | solution.py:734

commit v3 on v2

--- a/solution.py
+++ b/solution.py
@@ -18,14 +18,16 @@
 HB = 384
 D = NB * FB
 N_SEM = 320
+FEW = 32
+REACH = (4, 2)
 ORDER = (
-    0, 34, 1, 45, 17, 18, 35, 46, 9, 3, 2, 39, 36, 11, 10, 20, 4, 47, 13, 5, 26, 38, 12, 56, 37, 19, 15, 44,
-    14, 7, 6, 50, 49, 27, 48, 28, 40, 22, 21, 16, 43, 57, 55, 41, 52, 42, 51, 8, 59, 30, 29, 58, 60, 62, 23,
-    54, 24, 53, 63, 32, 31, 61, 64, 66, 25, 33, 149, 65, 116, 115, 86, 83, 67, 150, 88, 87, 119, 151, 68, 85,
-    152, 110, 136, 133, 153, 132, 107, 104, 122, 112, 111, 134, 91, 121, 109, 94, 139, 69, 138, 97, 120, 93,
-    108, 117, 100, 137, 92, 106, 70, 123, 101, 84, 80, 96, 125, 154, 105, 124, 95, 128, 141, 103, 82, 142,
-    140, 99, 155, 156, 72, 73, 102, 145, 127, 98, 118, 113, 81, 77, 126, 76, 130, 143, 71, 79, 75, 135, 147,
-    144, 114, 78, 157, 74, 89, 129, 159, 158, 146, 131, 160, 148, 90,
+    34, 47, 0, 1, 17, 35, 48, 18, 2, 3, 36, 20, 19, 60, 5, 49, 38, 4, 21, 9, 22, 61, 7, 39, 6, 26, 66, 37, 70,
+    50, 64, 23, 52, 8, 15, 44, 24, 41, 40, 10, 11, 51, 46, 28, 68, 27, 62, 42, 25, 53, 45, 12, 14, 13, 16, 43,
+    54, 31, 32, 63, 65, 58, 56, 67, 69, 29, 55, 71, 57, 30, 33, 72, 74, 59, 73, 123, 126, 130, 127, 157, 78,
+    88, 158, 159, 160, 144, 118, 90, 112, 140, 102, 99, 80, 120, 133, 85, 128, 114, 124, 104, 147, 115, 75,
+    101, 129, 94, 142, 87, 81, 109, 117, 91, 119, 146, 150, 141, 83, 84, 96, 77, 161, 111, 93, 100, 105, 145,
+    131, 116, 132, 107, 162, 97, 95, 136, 149, 125, 148, 103, 108, 113, 164, 153, 76, 92, 121, 163, 134, 143,
+    152, 106, 110, 138, 79, 89, 135, 165, 151, 122, 155, 86, 82, 167, 137, 154, 166, 139, 98, 156, 168,
 )
 
 
@@ -46,12 +48,12 @@
     patches, gain, w1in, ubias, w2in, dbias, cot,
     mixed_o, pgrad_o, gaing_o, dw1_o, ubg_o, dw2_o, dbg_o,
     XT, XN, CT, W1, W2, W1H, W2H,
-    GIN, UIN, DIN, GA, UB, BC, GW, MI,
+    GIN, UIN, DIN, GA, GF, UB, BC, GW, MI,
     PRE, SL, HG, HID, PG, HIDR, PGR,
-    MX, MXS, MXP, MXM, MXT,
-    NG, NGS, NGP, NGM, NGT,
-    G1, G1Y, G1X, G1T, G1F,
-    G2, G2Y, G2X, G2T, G2F,
+    MX, MXS, MXP, MXM, MXT, MXY,
+    NG, NGS, NGP, NGM, NGT, NGY,
+    G1, G1Y, G1K, G1X, G1T, G1F,
+    G2, G2Y, G2K, G2X, G2T, G2F,
     ST, STS, STZ, STT,
     MS, RM, UT, FU, GT, GTX, GTY,
     MO, PO, GO, UO, DO,
@@ -99,6 +101,7 @@
     for peer in peers:
         pl.semaphore_signal(barrier, inc=1, device_id=peer, device_id_type=MESH)
 
+    reach = REACH
     ids = {}
     made = {}
     seen = set()
@@ -160,13 +163,26 @@
         def relay(s, n, way):
             b, to, part = (zb(-n, k), zp, lo) if way == "p" else (zb(n, k), zm, hi)
             got(tag(t, way, n, s))
-            src = A.at[s, b] if n < 3 else A.at[s, b, part]
-            send(tag(t, way, n + 1, s), src, src, to)
+            if n < reach[s]:
+                src = A.at[s, b] if n < 3 else A.at[s, b, part]
+                send(tag(t, way, n + 1, s), src, src, to)
+            if not s and n > reach[1]:
+                send(tag(t, "y", way), A.at[0, b], A.at[1, b], tdev)
             send(tag(t, "sib", way, n, s), A.at[s, b], A.at[s, b], sib)
+
+        def across(way):
+            b = zb(-3, k) if way == "p" else zb(3, k)
+            got(tag(t, "y", way))
+            send(tag(t, "sib", way, 3, 1), A.at[1, b], A.at[1, b], sib)
 
         def last(s):
             b4 = zb(4, k)
-            got(tag(t, "p4", s), tag(t, "m4", s))
+            if s and reach[1] < 4:
+                got(tag(t, "y"))
+            else:
+                got(tag(t, "p4", s), tag(t, "m4", s))
+            if not s and reach[1] < 4:
+                send(tag(t, "y"), A.at[0, b4], A.at[1, b4], tdev)
             send(tag(t, "sib4", s), A.at[s, b4], A.at[s, b4], sib)
 
         task(t + "T", edge)
@@ -174,7 +190,10 @@
             task(tag(t, "f", s), functools.partial(first, s), t + "T")
             for n in range(1, 4):
                 for way in "pm":
-                    task(tag(t, way, n, s), functools.partial(relay, s, n, way))
+                    if n <= reach[s]:
+                        task(tag(t, way, n, s), functools.partial(relay, s, n, way))
+                    else:
+                        task(tag(t, way, n, s), functools.partial(across, way))
             task(tag(t, "l", s), functools.partial(last, s))
 
     def tokens_here(t, s):
@@ -182,6 +201,7 @@
             got(tag(t, "sib", n, s))
 
     lo, hi = pl.ds(0, FB // 2), pl.ds(FB // 2, FB // 2)
+    few, most = (pl.ds(0, FEW), pl.ds(FEW, FEW)), pl.ds(2 * FEW, FB - 2 * FEW)
     r0, rt, rq = wb(0, y), wb(0, yt), wb(0, yq)
 
     def gather_panel(t, WH, W):
@@ -230,7 +250,12 @@
         def last():
             b = wb(2, y)
             got(t + "P2+", t + "P2-")
-            send(t + "Y3", W.at[b], W.at[b], hdev)
+            send(t + "Y3", W.at[b, most], W.at[b, most], hdev)
+
+        def aside(j):
+            b, name, way, to, part = (wb(1, yh), "Y2", "Z-", xm, few[0]) if j > 0 else (wb(-1, yh), "Y1", "Z+", xp, few[1])
+            got(t + name)
+            send(t + way, W.at[b, part], W.at[b, part], to)
 
         task(t + "s", start)
         task(t + "0", spread0, t + "s")
@@ -240,9 +265,11 @@
             for way in "+-":
                 task(t + n + way, functools.partial(relay, n, yy, way))
         task(t + "l", last)
+        task(t + "z1", functools.partial(aside, 1))
+        task(t + "z2", functools.partial(aside, -1))
 
     def panel_here(t):
-        got(*(t + n for n in ("Q2+", "Q2-", "R2+", "R2-", "Y0", "Y1", "Y2", "Y3")))
+        got(*(t + n for n in ("Q2+", "Q2-", "R2+", "R2-", "Y0", "Y1", "Y2", "Y3", "Z+", "Z-")))
 
     gather_tokens("X", XT)
     gather_tokens("C", CT)
@@ -286,14 +313,23 @@
     def gain_column(kk, zz):
         return jnp.broadcast_to(GA[kk, zz], (8, 256)).T[:FB, 0:1]
 
+    def gain_lanes(part):
+        got("gas")
+
+        def block(b, carry):
+            GF[b] = jnp.broadcast_to(gain_column(rem(b, 2), b // 2), (FB, 128))
+            return carry
+
+        lax.fori_loop(part * 4, part * 4 + 4, block, 0)
+
     def normalise(part):
-        got("gas", "ub")
+        got("ub")
 
         def block(b, carry):
-            column = gain_column(rem(b, 2), b // 2)
+            wide = jnp.concatenate([GF[b]] * 2, axis=1)
             for slot in range(2):
                 v = (XT[slot, b].astype(F32) - MI[slot, 0:1]) * MI[slot, 1:2]
-                XN[slot, b] = (v * column).astype(BF)
+                XN[slot, b] = (v * wide).astype(BF)
             return carry
 
         lax.fori_loop(part * 4, part * 4 + 4, block, 0)
@@ -301,7 +337,8 @@
     task("st0", functools.partial(statistics, 0), "Xl0")
     task("st1", functools.partial(statistics, 1), "Xl1")
     for part in range(4):
-        task(tag("nm", part), functools.partial(normalise, part), "st0", "st1", "gb")
+        task(tag("gf", part), functools.partial(gain_lanes, part), "gb")
+        task(tag("nm", part), functools.partial(normalise, part), "st0", "st1", tag("gf", part))
 
     GRP = 4
 
@@ -335,11 +372,11 @@
         lax.fori_loop(0, HB // CH, functools.partial(gelu_rows, slot), 0)
         HIDR[slot] = HID[slot].T
 
-    task("pre", first_product, "nm0", "nm1", "nm2", "nm3", "V0", "V1", "V2", "Vl", "VP+", "VP-", "VQ+", "VQ-", "VR+", "VR-")
+    task("pre", first_product, "nm0", "nm1", "nm2", "nm3", "V0", "V1", "V2", "Vl", "Vz1", "Vz2", "VP+", "VP-", "VQ+", "VQ-", "VR+", "VR-")
     task("ge0", functools.partial(gelu, 0), "pre")
     task("ge1", functools.partial(gelu, 1), "pre")
 
-    def scatter_tokens(t, W, A, M, S, RP, RN, RT, finish, *after):
+    def scatter_tokens(t, W, A, M, S, RP, RN, RT, RY, finish, *after):
         def make(j):
             if t == "M":
                 panel_here("U")
@@ -353,19 +390,29 @@
 
         def relay(j, slot):
             b = zb(j, k)
+            n = abs(j)
             got(tag(t, "s", j))
             total = M[slot, b].astype(F32) + S[j + 3, slot].astype(F32)
-            if j == 3 and slot == 0 or j in (1, 2):
-                got(tag(t, "+", j + 1, slot))
-                total = total + RP[slot, 3 - j].astype(F32)
-            if j == -3 and slot == 1 or j in (-1, -2):
-                got(tag(t, "-", 1 - j, slot))
-                total = total + RN[slot, 3 + j].astype(F32)
+            if not slot and n > reach[1]:
+                got(tag(t, "y", j))
+                total = total + RY[{4: 0, 3: 1, -3: 2}[j]].astype(F32)
+            if n + 1 < reach[slot] + (reach[slot] < 4):
+                sign, R = ("+", RP) if j > 0 else ("-", RN)
+                got(tag(t, sign, n + 1, slot))
+                total = total + R[slot, 3 - n].astype(F32)
             M[slot, b] = total.astype(BF)
-            if j > 0 and (j < 4 or slot == 0):
-                send(tag(t, "+", j, slot), M.at[slot, b], RP.at[slot, 4 - j], zp)
+            if n == 3 and slot == 0:
+                sign, R, part = ("+", RP, lo) if j > 0 else ("-", RN, hi)
+                got(tag(t, sign, 4, slot))
+                M[slot, b, part] = (total[part.start:part.start + part.size] + R[slot, 0, part].astype(F32)).astype(BF)
+            if n > reach[slot]:
+                send(tag(t, "y", j), M.at[slot, b], RY.at[{4: 0, 3: 1, -3: 2}[j]], tdev)
+            elif n == 4:
+                send(tag(t, "+4", slot), M.at[slot, b, lo], RP.at[slot, 0, lo], zp)
+                send(tag(t, "-4", slot), M.at[slot, b, hi], RN.at[slot, 0, hi], zm)
+            elif j > 0:
+                send(tag(t, "+", n, slot), M.at[slot, b], RP.at[slot, 4 - n], zp)
             else:
-                n = abs(j)
                 send(tag(t, "-", n, slot), M.at[slot, b], RN.at[slot, 4 - n], zm)
 
         def summed(slot):
@@ -405,13 +452,13 @@
         GT[0, :, 0:FB] = product
         for j in range(1, 4):
             send(tag("gx", j), GT.at[0], GTX.at[j], xdev(j))
-        correction = grad * gain_column(k, z) - sums[0:1] / D - normed * (sums[1:2] / D)
+        correction = grad * jnp.concatenate([GF[b0]] * 2, axis=1) - sums[0:1] / D - normed * (sums[1:2] / D)
         PO[...] = (CT[0, b0].astype(F32) + inv_std * correction).astype(BF)
         copy_in("po", PO, pgrad_o)
 
-    UDONE = ("U0", "U1", "U2", "Ul", "UP+", "UP-", "UQ+", "UQ-", "UR+", "UR-")
-    scatter_tokens("M", W2, HID, MX, MXS, MXP, MXM, MXT, finish_mixed, "ge0", "ge1", *UDONE)
-    scatter_tokens("N", W1, PG, NG, NGS, NGP, NGM, NGT, finish_grad, "sl0", "sl1")
+    UDONE = ("U0", "U1", "U2", "Ul", "Uz1", "Uz2", "UP+", "UP-", "UQ+", "UQ-", "UR+", "UR-")
+    scatter_tokens("M", W2, HID, MX, MXS, MXP, MXM, MXT, MXY, finish_mixed, "ge0", "ge1", *UDONE)
+    scatter_tokens("N", W1, PG, NG, NGS, NGP, NGM, NGT, NGY, finish_grad, "sl0", "sl1")
 
     def deliver(t, T0, T1, out):
         @pl.when(own)
@@ -441,7 +488,7 @@
         def _():
             rc(t + "f0", t + "q0", T0, out.at[k], sib).wait_send()
 
-    def scatter_panel(t, A, B, G, RY, RX, T, F, out, *after):
+    def scatter_panel(t, A, B, G, RY, RK, RX, T, F, out, *after):
         made_here = set()
 
         def make(*blocks):
@@ -455,7 +502,17 @@
 
         def hid(j):
             make((j, yh))
-            send(tag(t, "h", j), G.at[wb(j, yh)], RY.at[j + 1], hdev)
+            b = wb(j, yh)
+            if j == 2:
+                send(t + "k+", G.at[b, few[0]], RK.at[0], xp)
+                send(t + "k-", G.at[b, few[1]], RK.at[1], xm)
+                send(tag(t, "h", j), G.at[b, most], RY.at[3, most], hdev)
+                return
+            if j:
+                i, name = (0, "k+") if j > 0 else (1, "k-")
+                got(t + name)
+                G[b, few[i]] = (G[b, few[i]].astype(F32) + RK[i].astype(F32)).astype(BF)
+            send(tag(t, "h", j), G.at[b], RY.at[j + 1], hdev)
 
         def far(n, i, yy):
             make((2, yy))
@@ -468,7 +525,8 @@
         def add(j):
             b = wb(j, y)
             got(tag(t, "h", j))
-            G[b] = (G[b].astype(F32) + RY[j + 1].astype(F32)).astype(BF)
+            rows = most if j == 2 else pl.ds(0, FB)
+            G[b, rows] = (G[b, rows].astype(F32) + RY[j + 1, rows].astype(F32)).astype(BF)
 
         def near(n, i, yy, j):
             to, way, part = (xp, "+", lo) if j > 0 else (xm, "-", hi)
@@ -532,15 +590,14 @@
         task(t + "tt", total_t, *after)
         task(t + "f", final, t + "to", t + "tt")
 
-    scatter_panel("D", CT, HIDR, G2, G2Y, G2X, G2T, G2F, dw2_o, "ge0", "ge1", "Cl0", "Cl1")
-    scatter_panel("E", XN, PGR, G1, G1Y, G1X, G1T, G1F, dw1_o, "sl0", "sl1")
+    scatter_panel("D", CT, HIDR, G2, G2Y, G2K, G2X, G2T, G2F, dw2_o, "ge0", "ge1", "Cl0", "Cl1")
+    scatter_panel("E", XN, PGR, G1, G1Y, G1K, G1X, G1T, G1F, dw1_o, "sl0", "sl1")
 
     def gain_weight():
         def step(b, total):
-            column = gain_column(rem(b, 2), b // 2)
-            return total + (W1[b].astype(F32) * column).reshape(FB // 8, 8, HB).sum(0)
-
-        got("gas")
+            wide = jnp.concatenate([GF[b]] * 3, axis=1)
+            return total + (W1[b].astype(F32) * wide).reshape(FB // 8, 8, HB).sum(0)
+
         panel_here("V")
         gw = lax.fori_loop(0, NB, step, jnp.zeros((8, HB), F32))
         gw = jnp.broadcast_to(jnp.sum(gw, axis=0, keepdims=True), (8, HB))
@@ -573,7 +630,7 @@
         PGR[slot] = turned
         up_sums.append(jnp.sum(turned.astype(F32), axis=0, keepdims=True))
 
-    task("gw", gain_weight, "gb", "pre")
+    task("gw", gain_weight, "pre")
     task("hg", second_product, "Cl0", "Cl1", *UDONE)
     task("sl0", functools.partial(slope, 0), "hg", "ge0", "gw")
     task("sl1", functools.partial(slope, 1), "hg", "ge1", "gw")
@@ -697,12 +754,12 @@
     panel = vm((NB, FB, HB), BF)
     tile = vm((2, HB, TB), F32)
     ring = vm((2, 4, FB, TB), BF)
-    scatter_z = [tokens, vm((8, 2, FB, TB), BF), ring, ring, vm((FB, TB), BF)]
-    scatter_w = [panel, vm((5, FB, HB), BF), vm((3, 3, FB, HB), BF), vm((3, FB, HB), BF), vm((2, FB, HB), BF)]
+    scatter_z = [tokens, vm((8, 2, FB, TB), BF), ring, ring, vm((FB, TB), BF), vm((3, FB, TB), BF)]
+    scatter_w = [panel, vm((5, FB, HB), BF), vm((2, FEW, HB), BF), vm((3, 3, FB, HB), BF), vm((3, FB, HB), BF), vm((2, FB, HB), BF)]
     scratch = [
         tokens, tokens, tokens, panel, panel, vm((2, FB, HB), BF), vm((2, FB, HB), BF),
         vm((1, FB), F32), vm((6, 128), F32), vm((1, FB), F32),
-        vm((2, 8, 1, 256), F32), vm((3, 1, HB), F32), vm((HB, 128), F32), vm((HB, 128), F32), vm((2, 8, TB), F32),
+        vm((2, 8, 1, 256), F32), vm((NB, FB, 128), F32), vm((3, 1, HB), F32), vm((HB, 128), F32), vm((HB, 128), F32), vm((2, 8, TB), F32),
         tile, tile, tile, vm((2, HB, TB), BF), vm((2, HB, TB), BF), vm((2, TB, HB), BF), vm((2, TB, HB), BF),
         *scatter_z, *scatter_z, *scatter_w, *scatter_w,
         vm((3, 2, 2, TB), F32), vm((2, 2, TB), F32), vm((8, 2, 2, TB), F32), vm((2, TB), F32),

time: 97.1 us -> 90.6 us (0.933)
  Pallas kernels: 96.2 us -> 88.8 us
    pallas_call x1, Pallas kernels: 94.1 us -> 86.8 us  [on_device(): pl.pallas_call(functools.partial(kernel, scale), out_shape=results, in_sp...]
where the time goes in v3:
time: 90.6 us; the launch traced here: 89.6 us
  Pallas kernels  88.8 us (98%)
    pallas_call x1, Pallas kernels, on_device(): pl.pallas_call(functools.partial(kernel, scale), out_shape=results, in_sp...  86.8 us
    pallas_call x1, Pallas kernels, on_device(): pl.pallas_call(hand_over, out_shape=results, in_specs=[pl.BlockSpec(memor...  2.08 us

profile of v3, /device:TPU:2, one launch (start us, length us, event | category | flops | bytes accessed | tf_op | source)
XLA Modules:
  0.0 89.6 jit_solution(17178853878935053767)
XLA Ops:
  0.6 86.8 %mlp_block.1 = (bf16[192,256]{1,0:T(8,128)(2,1)}, bf16[192,256]{1,0:T(8,128)(2,1)}, f32[1,192]{1,0:T(1,128)}, bf16[192,768]{1,0:T(8,128)(2,1)}, f32[6,128]{1,0:T...) custom-call(bf16[192,256]{1,0:T(8,128)(2,1)} %bitcast.13, f32[1,192]{1,0:T(1,128)} %bitcast.16, ...), custom_call_target="tpu_custom_call" | custom-call | tf_op jit(solution)/shard_map/mlp_block/pallas_call | solution.py:777
  87.4 2.1 %hand_over.1 = (bf16[192,256]{1,0:T(8,128)(2,1)}, bf16[192,256]{1,0:T(8,128)(2,1)}, f32[1,192]{1,0:T(1,128)}, bf16[192,768]{1,0:T(8,128)(2,1)}, f32[6,128]{1,0:T...) custom-call(bf16[192,256]{1,0:T(8,128)(2,1)} %get-tuple-element.21.refs_0_, ...), custom_call_target="tpu_custom_call" | custom-call | tf_op jit(solution)/shard_map/hand_over/pallas_call | solution.py:791

commit v4 on v3

--- a/solution.py
+++ b/solution.py
@@ -300,7 +300,7 @@
         def step(b, total):
             return total + term(XT[slot, b].astype(F32)).reshape(FB // 8, 8, TB).sum(0)
 
-        total = lax.fori_loop(0, NB, step, jnp.zeros((8, TB), F32))
+        total = lax.fori_loop(0, NB, step, jnp.zeros((8, TB), F32), unroll=4)
         return jnp.sum(total, axis=0, keepdims=True)
 
     def statistics(slot):
@@ -332,7 +332,7 @@
                 XN[slot, b] = (v * wide).astype(BF)
             return carry
 
-        lax.fori_loop(part * 4, part * 4 + 4, block, 0)
+        lax.fori_loop(part * 4, part * 4 + 4, block, 0, unroll=2)
 
     task("st0", functools.partial(statistics, 0), "Xl0")
     task("st1", functools.partial(statistics, 1), "Xl1")
@@ -599,7 +599,7 @@
             return total + (W1[b].astype(F32) * wide).reshape(FB // 8, 8, HB).sum(0)
 
         panel_here("V")
-        gw = lax.fori_loop(0, NB, step, jnp.zeros((8, HB), F32))
+        gw = lax.fori_loop(0, NB, step, jnp.zeros((8, HB), F32), unroll=4)
         gw = jnp.broadcast_to(jnp.sum(gw, axis=0, keepdims=True), (8, HB))
         GW[...] = jnp.broadcast_to(gw.T[:, 0:1], (HB, 128))
 
@@ -623,7 +623,7 @@
 
     def slope(slot):
         zero = jnp.zeros((8, TB), F32)
-        first, second = lax.fori_loop(0, HB // CH, functools.partial(slope_rows, slot), (zero, zero))
+        first, second = lax.fori_loop(0, HB // CH, functools.partial(slope_rows, slot), (zero, zero), unroll=3)
         ST[0, slot, 0:1] = jnp.sum(first, axis=0, keepdims=True)
         ST[0, slot, 1:2] = jnp.sum(second, axis=0, keepdims=True)
         turned = PG[slot].T

time: 90.6 us -> 90.5 us (level)
  no operation moved by 1% of the time
where the time goes in v4:
time: 90.5 us; the launch traced here: 89.8 us
  Pallas kernels  89 us (98%)
    pallas_call x1, Pallas kernels, on_device(): pl.pallas_call(functools.partial(kernel, scale), out_shape=results, in_sp...  86.9 us
    pallas_call x1, Pallas kernels, on_device(): pl.pallas_call(hand_over, out_shape=results, in_specs=[pl.BlockSpec(memor...  2.08 us

profile of v4, /device:TPU:2, one launch (start us, length us, event | category | flops | bytes accessed | tf_op | source)
XLA Modules:
  0.0 89.8 jit_solution(16752886611129413664)
XLA Ops:
  0.6 86.9 %mlp_block.1 = (bf16[192,256]{1,0:T(8,128)(2,1)}, bf16[192,256]{1,0:T(8,128)(2,1)}, f32[1,192]{1,0:T(1,128)}, bf16[192,768]{1,0:T(8,128)(2,1)}, f32[6,128]{1,0:T...) custom-call(bf16[192,256]{1,0:T(8,128)(2,1)} %bitcast.13, f32[1,192]{1,0:T(1,128)} %bitcast.16, ...), custom_call_target="tpu_custom_call" | custom-call | tf_op jit(solution)/shard_map/mlp_block/pallas_call | solution.py:777
  87.5 2.1 %hand_over.1 = (bf16[192,256]{1,0:T(8,128)(2,1)}, bf16[192,256]{1,0:T(8,128)(2,1)}, f32[1,192]{1,0:T(1,128)}, bf16[192,768]{1,0:T(8,128)(2,1)}, f32[6,128]{1,0:T...) custom-call(bf16[192,256]{1,0:T(8,128)(2,1)} %get-tuple-element.21.refs_0_, ...), custom_call_target="tpu_custom_call" | custom-call | tf_op jit(solution)/shard_map/hand_over/pallas_call | solution.py:791
